TPU v7x, 768 devices: a whole 4x8x12 slice. The times are simulated.
768 devices in a mesh: comp: 4 (over x), tile: 24 (over z, core), sub: 8 (over y).
Axes of the slice: x: 4, y: 8, z: 12, core: 2. Of those that a mesh axis runs over, the one named last changes fastest.
Arguments:
- atm_flux: float32 [4, 4, 98304], P(None, 'comp', ('tile', 'sub')), may hold values from -6 to 6
- ocean_tracer: float32 [4, 80, 196608], P('comp', None, ('tile', 'sub')), may hold values from -6 to 6
- pair_atm: int32 [1536, 4], P(('tile', 'sub')), may hold values from 0 to 127
- pair_count: int32 [1536], P(('tile', 'sub')), may hold values from 1 to 4
- pair_weight: float32 [1536, 4, 128, 128], P(('tile', 'sub')), may hold values from -0.25 to 0.25
- neighbors: int32 [6, 196608], P(None, ('tile', 'sub')), may hold values from 0 to 196607, as said below
- level_count: int32 [196608], P(('tile', 'sub')), may hold values from 1 to 80
- diff_horizontal: float32 [80], replicated, may hold values from 0.01 to 0.15
- diff_vertical: float32 [79], replicated, may hold values from 0.02 to 0.24
Outputs:
- ocean_final: float32 [4, 80, 196608], P('comp', None, ('tile', 'sub'))
- atm_surface: float32 [4, 4, 98304], P(None, 'comp', ('tile', 'sub'))
Inputs may be any that keep to these rules, and one draw needn't show every extreme that they name: `pair_atm`: region index of an atmosphere block in the ocean block's own tile region: section, then position along the region's cells. `pair_count`: slots at and after this count are padding. `neighbors`: each entry is an ocean cell at most 128 places away from its own cell in the cell order.
All inputs are finite; a program needn't handle non-finite values.
Results may differ from a plain program's by a relative error of at most 0.000092.
Values sent between devices are 32-bit elements; how exact they have to be, the bound alone decides.
A program may use at most 64 MiB of HBM per device.

v0:
```python
import jax
import jax.numpy as jnp
from jax import lax
from jax.sharding import PartitionSpec as P

HALO = 128


def extended(cells, sides, width):
    for axis, dim in sides:
        count = lax.axis_size(axis)
        ends = count - 1
        head = lax.slice_in_dim(cells, 0, width, axis=dim)
        tail = lax.slice_in_dim(cells, cells.shape[dim] - width, cells.shape[dim], axis=dim)
        cells = jnp.concatenate(
            [
                lax.ppermute(tail, axis, [(i, (i + 1) % count) for i in range(ends)]),
                cells,
                lax.ppermute(head, axis, [((i + 1) % count, i) for i in range(ends)]),
            ],
            axis=dim,
        )
    return cells


def diffuse(values, active, centre_lo, count, positions, diff_horizontal, diff_vertical):
    centre = lax.slice_in_dim(values, centre_lo, centre_lo + count, axis=1)
    here = lax.slice_in_dim(active, centre_lo, centre_lo + count, axis=1)
    total = jnp.zeros_like(centre)
    for slot in range(positions.shape[0]):
        other = jnp.take(values, positions[slot], axis=1)
        other_active = jnp.take(active, positions[slot], axis=1)
        total = total + other_active * (other - centre)
    mixed = centre + diff_horizontal[:, None] * here * total
    upward = diff_vertical[:, None] * here[1:] * (mixed[1:] - mixed[:-1])
    edge = jnp.zeros((1, count), jnp.float32)
    return mixed + jnp.concatenate([upward, edge], 0) - jnp.concatenate([edge, upward], 0)


def local(
    atm_flux,
    ocean_tracer,
    pair_atm,
    pair_count,
    pair_weight,
    neighbors,
    level_count,
    diff_horizontal,
    diff_vertical,
):
    own_blocks = pair_atm.shape[0]
    block = pair_weight.shape[2]
    own_cells = own_blocks * block
    levels = ocean_tracer.shape[1]
    atm_cells = atm_flux.shape[2]
    everything = lax.all_gather(atm_flux, ("comp", "sub"), axis=1, tiled=True)
    chosen = lax.dynamic_index_in_dim(everything, lax.axis_index("comp"), 0, keepdims=False)
    tile_field = chosen.reshape(-1, block)
    live = (lax.broadcasted_iota(jnp.int32, pair_atm.shape, 1) < pair_count[:, None]).astype(
        jnp.float32
    )
    sources = tile_field[pair_atm] * live[:, :, None]
    forcing = jnp.einsum("gkij,gkj->gi", pair_weight, sources, precision=lax.Precision.HIGHEST)
    field = ocean_tracer[0].at[0].add(forcing.reshape(-1))
    start = lax.axis_index(("tile", "sub")) * own_cells
    level_iota = lax.broadcasted_iota(jnp.int32, (levels, 1), 0)
    near = neighbors - (start - HALO)
    count_wide = extended(level_count, ((("tile", "sub"), 0),), HALO)
    active_wide = (level_iota < count_wide[None, :]).astype(jnp.float32)
    for step in range(2):
        wide = extended(field, ((("tile", "sub"), 1),), HALO)
        field = diffuse(wide, active_wide, HALO, own_cells, near, diff_horizontal, diff_vertical)
    top = field[0].reshape(own_blocks, block)
    contrib = (
        jnp.einsum("gkij,gi->gkj", pair_weight, top, precision=lax.Precision.HIGHEST)
        * live[:, :, None]
    )
    sections = lax.axis_size("comp")
    subgroup = lax.axis_size("sub")
    region_blocks = sections * subgroup * (atm_cells // block)
    table = (
        pair_atm.reshape(-1)[:, None] == lax.broadcasted_iota(jnp.int32, (1, region_blocks), 1)
    ).astype(jnp.float32)
    partial_value = jnp.einsum(
        "pa,pc->ac", table, contrib.reshape(-1, block), precision=lax.Precision.HIGHEST
    )
    partial_value = partial_value.reshape(sections, subgroup, atm_cells)
    summed = lax.psum_scatter(partial_value, "sub", scatter_dimension=1, tiled=True)
    summed = summed.reshape(1, sections, atm_cells)
    surface = lax.all_to_all(summed, "comp", split_axis=1, concat_axis=0, tiled=True)
    return (field[None], surface)


def solution(mesh):
    in_specs = (
        P(None, "comp", ("tile", "sub")),
        P("comp", None, ("tile", "sub")),
        P(("tile", "sub"), None),
        P(("tile", "sub")),
        P(("tile", "sub"), None, None, None),
        P(None, ("tile", "sub")),
        P(("tile", "sub")),
        P(),
        P(),
    )
    out_specs = (P("comp", None, ("tile", "sub")), P(None, "comp", ("tile", "sub")))
    return jax.shard_map(local, mesh=mesh, in_specs=in_specs, out_specs=out_specs, check_vma=False)
```

profile of v0, /device:TPU:8, one launch (start us, length us, event | category | flops | bytes accessed | tf_op | source)
XLA Modules:
  0.0 291.0 jit_solution(7601981845441268617)
XLA Ops:
  8.1 55.3 %all_gather.3 = f32[4,32,512]{2,0,1:T(4,128)S(1)} all-gather(f32[4,1,512]{2,0,1:T(4,128)S(1)} %copy.40), channel_id=1, replica_groups=mesh['comp'=4,'tile'=24,'sub'=8] {'comp','sub'}, dimensions={1}, use_global_device_ids=true | all-gather | bytes 270336 | tf_op jit(solution)/shard_map/all_gather | solution.py:56
  85.2 4.0 %gather_fusion.1 = f32[1024,80]{1,0:T(8,128)} fusion(f32[80,1280]{0,1:T(8,128)S(1)} %fusion.1, s32[1024]{0:T(1024)S(1)} %fusion.33), kind=kCustom, calls=%fused_computation.clone | custom fusion | bytes 659456 | tf_op jit(solution)/shard_map/jit(_take)/gather | solution.py:32
  89.2 4.0 %gather_fusion.3 = f32[1024,80]{1,0:T(8,128)} fusion(f32[80,1280]{0,1:T(8,128)S(1)} %fusion.1, s32[1024]{0:T(1024)S(1)} %fusion.34), kind=kCustom, calls=%fused_computation.2.clone | custom fusion | bytes 659456 | tf_op jit(solution)/shard_map/jit(_take)/gather | solution.py:32
  93.3 4.0 %gather_fusion.5 = f32[1024,80]{1,0:T(8,128)} fusion(f32[80,1280]{0,1:T(8,128)S(1)} %fusion.1, s32[1024]{0:T(1024)S(1)} %fusion.35), kind=kCustom, calls=%fused_computation.4.clone | custom fusion | bytes 659456 | tf_op jit(solution)/shard_map/jit(_take)/gather | solution.py:32
  97.3 4.0 %gather_fusion.7 = f32[1024,80]{1,0:T(8,128)} fusion(f32[80,1280]{0,1:T(8,128)S(1)} %fusion.1, s32[1024]{0:T(1024)S(1)} %fusion.36), kind=kCustom, calls=%fused_computation.6.clone | custom fusion | bytes 659456 | tf_op jit(solution)/shard_map/jit(_take)/gather | solution.py:32
  101.3 4.0 %gather_fusion.9 = f32[1024,80]{1,0:T(8,128)} fusion(f32[80,1280]{0,1:T(8,128)S(1)} %fusion.1, s32[1024]{0:T(1024)S(1)} %fusion.37), kind=kCustom, calls=%fused_computation.8.clone | custom fusion | bytes 659456 | tf_op jit(solution)/shard_map/jit(_take)/gather | solution.py:32
  105.3 4.0 %gather_fusion.11 = f32[1024,80]{1,0:T(8,128)} fusion(f32[80,1280]{0,1:T(8,128)S(1)} %fusion.1, s32[1024]{0:T(1024)S(1)} %fusion.38), kind=kCustom, calls=%fused_computation.10.clone | custom fusion | bytes 659456 | tf_op jit(solution)/shard_map/jit(_take)/gather | solution.py:32
  110.5 4.0 %gather_fusion.2 = f32[1024,80]{1,0:T(8,128)} fusion(f32[80,1280]{0,1:T(8,128)S(1)} %pad_maximum_fusion, s32[1024]{0:T(1024)S(1)} %fusion.33), kind=kCustom, calls=%fused_computation.1.clone | custom fusion | bytes 659456 | tf_op jit(solution)/shard_map/jit(_take)/gather | solution.py:31
  114.5 4.0 %gather_fusion.4 = f32[1024,80]{1,0:T(8,128)} fusion(f32[80,1280]{0,1:T(8,128)S(1)} %pad_maximum_fusion, s32[1024]{0:T(1024)S(1)} %fusion.34), kind=kCustom, calls=%fused_computation.3.clone | custom fusion | bytes 659456 | tf_op jit(solution)/shard_map/jit(_take)/gather | solution.py:31
  118.5 4.1 %gather_fusion.6 = f32[1024,80]{1,0:T(8,128)} fusion(f32[80,1280]{0,1:T(8,128)S(1)} %pad_maximum_fusion, s32[1024]{0:T(1024)S(1)} %fusion.35), kind=kCustom, calls=%fused_computation.5.clone | custom fusion | bytes 659456 | tf_op jit(solution)/shard_map/jit(_take)/gather | solution.py:31
  122.6 4.0 %gather_fusion.8 = f32[1024,80]{1,0:T(8,128)} fusion(f32[80,1280]{0,1:T(8,128)S(1)} %pad_maximum_fusion, s32[1024]{0:T(1024)S(1)} %fusion.36), kind=kCustom, calls=%fused_computation.7.clone | custom fusion | bytes 659456 | tf_op jit(solution)/shard_map/jit(_take)/gather | solution.py:31
  126.6 4.0 %gather_fusion.10 = f32[1024,80]{1,0:T(8,128)} fusion(f32[80,1280]{0,1:T(8,128)S(1)} %pad_maximum_fusion, s32[1024]{0:T(1024)S(1)} %fusion.37), kind=kCustom, calls=%fused_computation.9.clone | custom fusion | bytes 659456 | tf_op jit(solution)/shard_map/jit(_take)/gather | solution.py:31
  130.6 4.0 %gather_fusion.12 = f32[1024,80]{1,0:T(8,128)} fusion(f32[80,1280]{0,1:T(8,128)S(1)} %pad_maximum_fusion, s32[1024]{0:T(1024)S(1)} %fusion.38), kind=kCustom, calls=%fused_computation.11.clone | custom fusion | bytes 659456 | tf_op jit(solution)/shard_map/jit(_take)/gather | solution.py:31
  134.7 4.2 %fusion.20 = f32[80,1024]{0,1:T(8,128)S(1)} fusion(f32[80,1024]{0,1:T(8,128)} %copy-done.2, f32[1024,80]{1,0:T(8,128)} %gather_fusion.12, f32[1024,80]{1,0:T(8,128)} %gather_fusion.10, f32[1024,80]{1,0:T(8,128)} %gather_fusion.8, f32[1024,80]{1,0:T(8,128)} %gather_fusion.6, f32[1024,80]{1,0:T(8,128)} %gather_fusion.4, f32[1024,80]{1,0:T(8,128)} %gather_fusion.2, ...), kind=kLoop, calls=%fused_computation.55 | loop fusion | flops 2621440 | bytes 4921664 | tf_op jit(solution)/shard_map/add | solution.py:34
  151.9 4.0 %gather_fusion.13 = f32[1024,80]{1,0:T(8,128)} fusion(f32[80,1280]{0,1:T(8,128)S(1)} %pad_maximum_fusion.1, s32[1024]{0:T(1024)S(1)} %fusion.33), kind=kCustom, calls=%fused_computation.12.clone | custom fusion | bytes 659456 | tf_op jit(solution)/shard_map/jit(_take)/gather | solution.py:31
  156.0 4.0 %gather_fusion.14 = f32[1024,80]{1,0:T(8,128)} fusion(f32[80,1280]{0,1:T(8,128)S(1)} %pad_maximum_fusion.1, s32[1024]{0:T(1024)S(1)} %fusion.34), kind=kCustom, calls=%fused_computation.13.clone | custom fusion | bytes 659456 | tf_op jit(solution)/shard_map/jit(_take)/gather | solution.py:31
  160.0 4.0 %gather_fusion.15 = f32[1024,80]{1,0:T(8,128)} fusion(f32[80,1280]{0,1:T(8,128)S(1)} %pad_maximum_fusion.1, s32[1024]{0:T(1024)S(1)} %fusion.35), kind=kCustom, calls=%fused_computation.14.clone | custom fusion | bytes 659456 | tf_op jit(solution)/shard_map/jit(_take)/gather | solution.py:31
  164.0 4.1 %gather_fusion.16 = f32[1024,80]{1,0:T(8,128)} fusion(f32[80,1280]{0,1:T(8,128)S(1)} %pad_maximum_fusion.1, s32[1024]{0:T(1024)S(1)} %fusion.36), kind=kCustom, calls=%fused_computation.15.clone | custom fusion | bytes 659456 | tf_op jit(solution)/shard_map/jit(_take)/gather | solution.py:31
  168.1 4.0 %gather_fusion.17 = f32[1024,80]{1,0:T(8,128)} fusion(f32[80,1280]{0,1:T(8,128)S(1)} %pad_maximum_fusion.1, s32[1024]{0:T(1024)S(1)} %fusion.37), kind=kCustom, calls=%fused_computation.16.clone | custom fusion | bytes 659456 | tf_op jit(solution)/shard_map/jit(_take)/gather | solution.py:31
  172.1 4.0 %gather_fusion.18 = f32[1024,80]{1,0:T(8,128)} fusion(f32[80,1280]{0,1:T(8,128)S(1)} %pad_maximum_fusion.1, s32[1024]{0:T(1024)S(1)} %fusion.38), kind=kCustom, calls=%fused_computation.17.clone | custom fusion | bytes 659456 | tf_op jit(solution)/shard_map/jit(_take)/gather | solution.py:31
  176.1 4.8 %fusion.7 = f32[80,1024]{0,1:T(8,128)S(1)} fusion(f32[1024,80]{1,0:T(8,128)} %gather_fusion.18, f32[1024,80]{1,0:T(8,128)} %gather_fusion.17, f32[1024,80]{1,0:T(8,128)} %gather_fusion.16, f32[1024,80]{1,0:T(8,128)} %gather_fusion.15, f32[1024,80]{1,0:T(8,128)} %gather_fusion.14, f32[1024,80]{1,0:T(8,128)} %gather_fusion.13, f32[79,1024]{0,1:T(8,128)} %copy-done.3, ...), kind=kLoop, calls=%fused_computation.36 | loop fusion | flops 2785280 | bytes 5245248 | tf_op jit(solution)/shard_map/add | solution.py:34
  185.2 86.8 %all-reduce.7.cloned.1.call-done = f32[4,8,512]{2,0,1:T(4,128)} async-done(((f32[4,8,512]{2,0,1:T(4,128)}), f32[4,8,512]{2,0,1:T(4,128)}) %all-reduce.7.cloned.1.call-update) | async-done | bytes 65552
  273.9 4.2 %all-to-all-start = ((f32[1,4,512]{2,0,1:T(1,128)}), f32[1,4,512]{2,0,1:T(1,128)S(1)}, u32[]{:S(2)}, u32[]{:S(2)}) async-start(f32[1,4,512]{2,0,1:T(1,128)} %copy.45), calls=%async_computation | async-start | bytes 16384 | tf_op jit(solution)/shard_map/all_to_all | solution.py:90
  279.1 4.4 %all-to-all-done = f32[1,4,512]{2,0,1:T(1,128)S(1)} async-done(((f32[1,4,512]{2,0,1:T(1,128)}), f32[1,4,512]{2,0,1:T(1,128)S(1)}, u32[]{:S(2)}, u32[]{:S(2)}) %all-to-all-start) | async-done | bytes 8224 | tf_op jit(solution)/shard_map/all_to_all | solution.py:90
  (82 shorter events, 44.3 us)
Async XLA Ops:
  7.2 59.7 %copy-start = (f32[8,4,128,128]{3,2,1,0:T(8,128)S(1)}, f32[8,4,128,128]{3,2,1,0:T(8,128)}, u32[]{:S(2)}) copy-start(f32[8,4,128,128]{3,2,1,0:T(8,128)} %param.17) | copy-start | bytes 6291460
  7.2 264.8 %all-reduce.7.cloned.1.call-start = ((), (), s32[]{:S(2)}) async-start(), calls=%async_computation.1 | async-start | bytes 131072
  66.2 11.4 %copy-start.7 = (s32[1024]{0:T(1024)S(1)}, s32[1024]{0:T(1024)}, u32[]{:S(2)}) copy-start(s32[1024]{0:T(1024)} %param.19) | copy-start | bytes 12292
  66.2 17.3 %copy-start.5 = (s32[6,1024]{1,0:T(8,128)S(1)}, s32[6,1024]{1,0:T(8,128)}, u32[]{:S(2)}) copy-start(s32[6,1024]{1,0:T(8,128)} %param.18) | copy-start | bytes 73732
  71.7 13.3 %copy-start.2 = (f32[80,1024]{0,1:T(8,128)}, f32[80,1024]{0,1:T(8,128)S(1)}, u32[]{:S(2)}) copy-start(f32[80,1024]{0,1:T(8,128)S(1)} %scatter-add.4) | copy-start | bytes 983044
  71.7 37.6 %collective-permute-start.2 = (f32[80,128]{0,1:T(8,128)S(1)}, f32[80,128]{0,1:T(8,128)S(1)}, u32[]{:S(2)}, u32[]{:S(2)}) collective-permute-start(f32[80,128]{0,1:T(8,128)S(1)} %get-tuple-element.27), channel_id=1, source_target_pairs={{0,1},{1,2},{2,3},{3,4},{4,5},{5,6},{6,7},{7,8},{8,9},{9,10},{10,1... | collective-permute-start | bytes 122888 | tf_op jit(solution)/shard_map/ppermute | solution.py:17
  73.6 35.7 %collective-permute-start.3 = (f32[80,128]{0,1:T(8,128)S(1)}, f32[80,128]{0,1:T(8,128)}, u32[]{:S(2)}, u32[]{:S(2)}) collective-permute-start(f32[80,128]{0,1:T(8,128)S(1)} %get-tuple-element.28), channel_id=1, source_target_pairs={{1,0},{2,1},{3,2},{4,3},{5,4},{6,5},{7,6},{8,7},{9,8},{10,9},{11,1... | collective-permute-start | bytes 122888 | tf_op jit(solution)/shard_map/ppermute | solution.py:19
  77.6 6.1 %collective-permute-start = (s32[128]{0:T(128)S(1)}, s32[128]{0:T(128)S(1)}, u32[]{:S(2)}, u32[]{:S(2)}) collective-permute-start(s32[128]{0:T(128)S(1)} %get-tuple-element.35), channel_id=1, source_target_pairs={{0,1},{1,2},{2,3},{3,4},{4,5},{5,6},{6,7},{7,8},{8,9},{9,10},{10,1... | collective-permute-start | bytes 1544 | tf_op jit(solution)/shard_map/ppermute | solution.py:17
  79.5 5.4 %collective-permute-start.1 = (s32[128]{0:T(128)S(1)}, s32[128]{0:T(128)S(1)}, u32[]{:S(2)}, u32[]{:S(2)}) collective-permute-start(s32[128]{0:T(128)S(1)} %get-tuple-element.36), channel_id=1, source_target_pairs={{1,0},{2,1},{3,2},{4,3},{5,4},{6,5},{7,6},{8,7},{9,8},{10,9},{11,1... | collective-permute-start | bytes 1544 | tf_op jit(solution)/shard_map/ppermute | solution.py:19
  130.6 4.0 %copy-start.8 = (f32[80]{0:T(128)S(1)}, f32[80]{0:T(128)}, u32[]{:S(2)}) copy-start(f32[80]{0:T(128)} %param.20) | copy-start | bytes 964
  134.7 4.2 %copy-start.9 = (f32[79]{0:T(128)S(1)}, f32[79]{0:T(128)}, u32[]{:S(2)}) copy-start(f32[79]{0:T(128)} %param.21) | copy-start | bytes 952
  138.9 0.8 copy-start.1
  138.9 8.2 %copy-start.6 = (s32[8,4]{0,1:T(4,128)S(1)}, s32[8,4]{0,1:T(4,128)}, u32[]{:S(2)}) copy-start(s32[8,4]{0,1:T(4,128)} %param.15) | copy-start | bytes 388
  139.7 0.8 copy-start.3
  140.5 0.8 copy-start.4
  141.3 6.1 %collective-permute-start.4 = (f32[80,128]{0,1:T(8,128)S(1)}, f32[80,128]{0,1:T(8,128)S(1)}, u32[]{:S(2)}, u32[]{:S(2)}) collective-permute-start(f32[80,128]{0,1:T(8,128)S(1)} %get-tuple-element.25), channel_id=1, source_target_pairs={{0,1},{1,2},{2,3},{3,4},{4,5},{5,6},{6,7},{7,8},{8,9},{9,10},{10,1... | collective-permute-start | bytes 122888 | tf_op jit(solution)/shard_map/ppermute | solution.py:17
  144.1 6.8 %collective-permute-start.5 = (f32[80,128]{0,1:T(8,128)S(1)}, f32[80,128]{0,1:T(8,128)}, u32[]{:S(2)}, u32[]{:S(2)}) collective-permute-start(f32[80,128]{0,1:T(8,128)S(1)} %get-tuple-element.26), channel_id=1, source_target_pairs={{1,0},{2,1},{3,2},{4,3},{5,4},{6,5},{7,6},{8,7},{9,8},{10,9},{11,1... | collective-permute-start | bytes 122888 | tf_op jit(solution)/shard_map/ppermute | solution.py:19
  273.9 9.6 %all-to-all-start = ((f32[1,4,512]{2,0,1:T(1,128)}), f32[1,4,512]{2,0,1:T(1,128)S(1)}, u32[]{:S(2)}, u32[]{:S(2)}) async-start(f32[1,4,512]{2,0,1:T(1,128)} %copy.45), calls=%async_computation | async-start | bytes 16384 | tf_op jit(solution)/shard_map/all_to_all | solution.py:90
Sparse Core Ops, SparseCore 0:
  184.0 87.9 all-reduce.6
where the time goes:
time: 292 us; the launch traced here: 291 us
  waiting for transfers between devices  96 us (33%)
  local copies, waits for them, and re-layouts  85.2 us (29%)
  blocking collectives  55.3 us (19%)
  starting transfers between devices  21.8 us (7%)
  between operations  14.4 us (5%)
  other arithmetic  14.2 us (5%)
  matrix products  4.01 us (1%)
    unnamed x2, waiting for transfers between devices  86.8 us
    all_gather x1, blocking collectives, local(): everything = lax.all_gather(atm_flux, ('comp', 'sub'), axis=1, tiled=True)  55.3 us
    gather x12, local copies, waits for them, and re-layouts, diffuse(): other = jnp.take(values, positions[slot], axis=1)  48.4 us
    gather x6, local copies, waits for them, and re-layouts, diffuse(): other_active = jnp.take(active, positions[slot], axis=1)  24.1 us
    ppermute x3, starting transfers between devices, extended(): lax.ppermute(head, axis, [((i + 1) % count, i) for i in range(ends)])  10.9 us
    add x2, other arithmetic, diffuse(): mixed = centre + diff_horizontal[:, None] * here * total  9 us
    unnamed x26, local copies, waits for them, and re-layouts  6.72 us
    ppermute x3, starting transfers between devices, extended(): lax.ppermute(tail, axis, [(i, (i + 1) % count) for i in range(ends)])  6.58 us
  transfers between devices with their start and end apart: 8, of which 5 were waited for; matrix products, arithmetic and copies ran while one was open for 9% of the time, Pallas kernels for 0%

commit v1 on v0

v1 whole, which is shorter than its diff:
```python
import functools

import jax
import jax.numpy as jnp
from jax import lax
from jax.experimental import pallas as pl
from jax.experimental.pallas import tpu as pltpu
from jax.sharding import PartitionSpec as P

MESH = pl.DeviceIdType.MESH
B = 128
F32 = jnp.float32
BF16 = jnp.bfloat16


def split(x):
    hi = x.astype(BF16)
    lo = (x - hi.astype(F32)).astype(BF16)
    return hi, lo


def relax(centre, total, count, depth, dh, dv):
    k = lax.broadcasted_iota(jnp.int32, centre.shape, 0)
    rows = centre.shape[0]
    mixed = centre + jnp.where(k < depth, dh, 0.0) * (total - count * centre)
    below = pltpu.roll(mixed, rows - 1, 0)
    flux = jnp.where(k + 1 < depth, dv, 0.0) * (below - mixed)
    above = jnp.where(k > 0, pltpu.roll(flux, 1, 0), 0.0)
    return mixed + flux - above


def kernel(
    nc, nt, ns, nb, levels,
    atm, tracer, pair_atm, pair_count, weight, neighbors, depth_own, diff_h, diff_v,
    ocean, surface,
    atm_all, v0, v1, x1, x2, xt1, xt2, w, near, depth_l, depth_o, depth_r, depth, table, count,
    dh, dv, adj, adj_edge, force, contrib, contrib3, parts, arrived, vt1,
    sem_load, sem_atm, sem_halo_s, sem_halo_r, sem_force_s, sem_force_r, sem_surf, sem_out,
):
    c, t, s = lax.axis_index("comp"), lax.axis_index("tile"), lax.axis_index("sub")
    own = nb * B
    wide = own + 4 * B
    pairs = nb // 2
    peers = nc * ns
    line = t * ns + s
    right, left = lax.rem(line + 1, nt * ns), lax.rem(line + nt * ns - 1, nt * ns)
    to_right = (c, right // ns, lax.rem(right, ns))
    to_left = (c, left // ns, lax.rem(left, ns))
    slot = c * ns + s

    def peer(d):
        pc = lax.rem(c + d // ns, nc)
        ps = lax.rem(s + lax.rem(d, ns), ns)
        return pc, ps

    barrier = pltpu.get_barrier_semaphore()

    def greet(d, carry):
        pc, ps = peer(d)
        pl.semaphore_signal(barrier, inc=1, device_id=(pc, t, ps), device_id_type=MESH)
        return carry

    lax.fori_loop(1, peers, greet, 0)
    for other in (to_right, to_left):
        pl.semaphore_signal(barrier, inc=1, device_id=other, device_id_type=MESH)

    loads = [
        pltpu.make_async_copy(neighbors, near.at[:, B : B + own], sem_load.at[0]),
        pltpu.make_async_copy(depth_own, depth_o, sem_load.at[1]),
        pltpu.make_async_copy(tracer, v0.at[:, 2 * B : 2 * B + own], sem_load.at[2]),
        pltpu.make_async_copy(weight, w, sem_load.at[3]),
    ]
    for copy in loads:
        copy.start()

    dh[...] = jnp.broadcast_to(diff_h[...], (B, levels)).T
    dv[0 : levels, :] = jnp.broadcast_to(diff_v[...], (B, levels)).T

    lane = lax.broadcasted_iota(jnp.int32, (8, B), 1)
    row = jnp.full((8, B), -1, jnp.int32)
    for g in range(nb):
        for k in range(4):
            goal = jnp.where(k < pair_count[0, g], pair_atm[g, k], -1)
            row = jnp.where(lane % 32 == g * 4 + k, goal, row)
    row = jnp.where(lane < 96, row, -1)
    blocks = peers * 4
    table[...] = jnp.where(
        lax.broadcasted_iota(jnp.int32, (blocks, B), 0) == row[0:1], 1.0, 0.0
    ).astype(BF16)

    start = line * own
    source = lax.broadcasted_iota(jnp.int32, (B, B), 0)

    def quadrant(target, base):
        acc = jnp.zeros((B, B), F32)
        for p in range(6):
            at = near[p : p + 1, (target - 1) * B : target * B] - (start - 2 * B + base * B)
            acc = acc + jnp.where(at == source, 1.0, 0.0)
        return acc.astype(BF16)

    loads[0].wait()
    for q in range(pairs):
        a = 2 + 2 * q
        for i in range(3):
            adj[q, i * B : (i + 1) * B, 0:B] = quadrant(a, a - 1 + i)
            adj[q, (i + 1) * B : (i + 2) * B, B : 2 * B] = quadrant(a + 1, a + i)
        adj[q, 3 * B : 4 * B, 0:B] = jnp.zeros((B, B), BF16)
        adj[q, 0:B, B : 2 * B] = jnp.zeros((B, B), BF16)

    pl.semaphore_wait(barrier, peers - 1 + 2)

    def send_atm(d, carry):
        pc, ps = peer(d)
        pltpu.make_async_remote_copy(
            src_ref=atm.at[pc], dst_ref=atm_all.at[slot], send_sem=sem_atm.at[0], recv_sem=sem_atm.at[1],
            device_id=(pc, t, ps), device_id_type=MESH,
        ).start()
        return carry

    lax.fori_loop(1, peers, send_atm, 0)
    pltpu.make_async_copy(atm.at[c], atm_all.at[slot], sem_atm.at[1]).start()

    halo = []
    plan = [
        (neighbors.at[:, own - B : own], near.at[:, 0:B], to_right),
        (neighbors.at[:, 0:B], near.at[:, B + own : 2 * B + own], to_left),
        (depth_own, depth_l, to_right),
        (depth_own, depth_r, to_left),
        (tracer.at[:, own - 2 * B : own], v0.at[:, 0 : 2 * B], to_right),
        (tracer.at[:, 0 : 2 * B], v0.at[:, 2 * B + own : wide], to_left),
    ]
    for i, (src, dst, other) in enumerate(plan):
        copy = pltpu.make_async_remote_copy(
            src_ref=src, dst_ref=dst, send_sem=sem_halo_s.at[i], recv_sem=sem_halo_r.at[i],
            device_id=other, device_id_type=MESH,
        )
        copy.start()
        halo.append(copy)

    loads[1].wait()
    for g in range(nb):
        depth[:, (2 + g) * B : (3 + g) * B] = jnp.broadcast_to(depth_o[g : g + 1, :], (8, B))

    def prepare(values, store, lo, n):
        d = depth[0:1, lo : lo + n]
        rows = values.shape[0]
        k = lax.broadcasted_iota(jnp.int32, (rows, n), 0)
        hi, low = split(jnp.where(k < d, values, 0.0))
        store[0:rows, lo : lo + n] = hi
        store[rows : 2 * rows, lo : lo + n] = low

    def prepare_first(lo, n):
        prepare(v0[:, lo : lo + n], x1, lo, n)
        k = lax.broadcasted_iota(jnp.int32, (levels, n), 0)
        x1[2 * levels : 3 * levels, lo : lo + n] = jnp.where(k < depth[0:1, lo : lo + n], 1.0, 0.0).astype(BF16)

    groups = [(2 * B + 2 * B * q, 2 * B, adj.at[q]) for q in range(pairs)]
    edges = [(B, B, adj_edge.at[0]), (2 * B + own, B, adj_edge.at[1])]

    def first(lo, n, matrix):
        r = jnp.dot(x1[:, lo - B : lo + n + B], matrix[...], preferred_element_type=F32)
        cnt = r[2 * levels : 3 * levels]
        count[:, lo : lo + n] = cnt
        new = relax(
            v0[:, lo : lo + n], r[0:levels] + r[levels : 2 * levels], cnt, depth[0:1, lo : lo + n],
            jnp.concatenate([dh[...]] * (n // B), 1), jnp.concatenate([dv[...]] * (n // B), 1),
        )
        v1[:, lo : lo + n] = new
        prepare(new, x2, lo, n)

    def second(lo, n, matrix):
        r = jnp.dot(x2[:, lo - B : lo + n + B], matrix[...], preferred_element_type=F32)
        return relax(
            v1[:, lo : lo + n], r[0:levels] + r[levels : 2 * levels], count[:, lo : lo + n], depth[0:1, lo : lo + n],
            jnp.concatenate([dh[...]] * (n // B), 1), jnp.concatenate([dv[...]] * (n // B), 1),
        )

    loads[2].wait()
    for q in range(pairs):
        prepare_first(2 * B + 2 * B * q, 2 * B)
    for group in groups[1:-1]:
        first(*group)
    for i in range(4):
        halo[i].wait_recv()
    for i in range(2):
        depth[:, i * B : (i + 1) * B] = jnp.broadcast_to(depth_l[nb - 2 + i : nb - 1 + i, :], (8, B))
        depth[:, (2 + nb + i) * B : (3 + nb + i) * B] = jnp.broadcast_to(depth_r[i : i + 1, :], (8, B))
        target = 1 + i * (nb + 1)
        for j in range(3):
            adj_edge[i, j * B : (j + 1) * B, :] = quadrant(target, target - 1 + j)
    for i in range(4, 6):
        halo[i].wait_recv()
    prepare_first(0, 2 * B)
    prepare_first(2 * B + own, 2 * B)
    first(*groups[0])
    first(*groups[-1])
    for edge in edges:
        first(*edge)

    loads[3].wait()
    pltpu.make_async_copy(atm_all, atm_all, sem_atm.at[1]).wait()

    def forcing(g):
        acc = jnp.zeros((B, B), F32)
        for k in range(4):
            a = pair_atm[g, k]
            live = jnp.where(k < pair_count[0, g], 1.0, 0.0)
            acc = acc + w[g, k] * (atm_all[a // 4, pl.ds(lax.rem(a, 4), 1), :] * live)
        force[0:1, (2 + g) * B : (3 + g) * B] = jnp.sum(acc.T, axis=0, keepdims=True)

    def send_force(i, lo, goal, other):
        copy = pltpu.make_async_remote_copy(
            src_ref=force.at[:, lo : lo + 2 * B], dst_ref=force.at[:, goal : goal + 2 * B],
            send_sem=sem_force_s.at[i], recv_sem=sem_force_r.at[i], device_id=other, device_id_type=MESH,
        )
        copy.start()
        return copy

    for g in (nb - 2, nb - 1):
        forcing(g)
    copies = [send_force(0, own, 0, to_right)]
    for g in (0, 1):
        forcing(g)
    copies.append(send_force(1, 2 * B, 2 * B + own, to_left))
    for g in range(2, nb - 2):
        forcing(g)

    outs = []
    for group in groups:
        lo, n, _ = group
        ocean[:, lo - 2 * B : lo - 2 * B + n] = second(*group)

    for copy in copies:
        copy.wait_recv()

    k8 = lax.broadcasted_iota(jnp.int32, (8, wide), 0)
    top = v0[0:8, :] + jnp.where(k8 == 0, jnp.broadcast_to(force[...], (8, wide)), 0.0)
    prepare(top, xt1, 0, wide)

    def top_step(centre, store, lo, n, matrix):
        r = jnp.dot(store[:, lo - B : lo + n + B], matrix[...], preferred_element_type=F32)
        return relax(
            centre, r[0:8] + r[8:16], count[0:8, lo : lo + n], depth[0:1, lo : lo + n],
            jnp.concatenate([dh[0:8, :]] * (n // B), 1), jnp.concatenate([dv[0:8, :]] * (n // B), 1),
        )

    for lo, n, matrix in groups + edges:
        new = top_step(top[:, lo : lo + n], xt1, lo, n, matrix)
        vt1[:, lo : lo + n] = new
        prepare(new, xt2, lo, n)
    for lo, n, matrix in groups:
        new = top_step(vt1[:, lo : lo + n], xt2, lo, n, matrix)
        k = lax.broadcasted_iota(jnp.int32, (8, n), 0)
        here = slice(lo - 2 * B, lo - 2 * B + n)
        ocean[0:8, here] = jnp.where(k < 3, new, ocean[0:8, here])
        for half in range(n // B):
            g = (lo - 2 * B) // B + half
            column = jnp.broadcast_to(new[0:1, half * B : (half + 1) * B], (B, B)).T
            for k in range(4):
                contrib[4 * g + k : 4 * g + k + 1, :] = jnp.sum(w[g, k] * column, axis=0, keepdims=True)

    rest = contrib[...]
    for i in range(3):
        part = rest.astype(BF16)
        contrib3[32 * i : 32 * (i + 1), :] = part
        rest = rest - part.astype(F32)
    contrib3[96:128, :] = jnp.zeros((32, B), BF16)
    summed = jnp.dot(table[...], contrib3[...], preferred_element_type=F32)
    for i in range(peers):
        parts[i] = summed[4 * i : 4 * (i + 1)]

    def send_part(d, carry):
        pc, ps = peer(d)
        pltpu.make_async_remote_copy(
            src_ref=parts.at[pc * ns + ps], dst_ref=arrived.at[slot], send_sem=sem_surf.at[0], recv_sem=sem_surf.at[1],
            device_id=(pc, t, ps), device_id_type=MESH,
        ).start()
        return carry

    lax.fori_loop(1, peers, send_part, 0)
    pltpu.make_async_copy(parts.at[slot], arrived.at[slot], sem_surf.at[1]).start()
    pltpu.make_async_copy(arrived, arrived, sem_surf.at[1]).wait()
    for i in range(nc):
        surface[i] = jnp.sum(arrived[i * ns : (i + 1) * ns], axis=0)

    sent = pl.ds(0, peers - 1)
    pltpu.make_async_copy(atm_all.at[sent], atm_all.at[sent], sem_atm.at[0]).wait()
    pltpu.make_async_copy(parts.at[sent], parts.at[sent], sem_surf.at[0]).wait()
    for copy in halo + copies:
        copy.wait_send()


def solution(mesh):
    nc, nt, ns = mesh.shape["comp"], mesh.shape["tile"], mesh.shape["sub"]

    def local(atm_flux, ocean_tracer, pair_atm, pair_count, pair_weight, neighbors, level_count, diff_h, diff_v):
        tracers, _, atm_cells = atm_flux.shape
        _, levels, own = ocean_tracer.shape
        nb = own // B
        wide = own + 4 * B
        peers = nc * ns
        vm = pl.BlockSpec(memory_space=pltpu.VMEM)
        sm = pl.BlockSpec(memory_space=pltpu.SMEM)
        anywhere = pl.BlockSpec(memory_space=pl.ANY)
        dma = pltpu.SemaphoreType.DMA
        ocean, surface = pl.pallas_call(
            functools.partial(kernel, nc, nt, ns, nb, levels),
            out_shape=(
                jax.ShapeDtypeStruct((levels, own), F32),
                jax.ShapeDtypeStruct((tracers, atm_cells // B, B), F32),
            ),
            in_specs=[anywhere, anywhere, sm, sm, anywhere, anywhere, anywhere, vm, vm],
            out_specs=(vm, vm),
            scratch_shapes=[
                pltpu.VMEM((peers, 4, B), F32),
                pltpu.VMEM((levels, wide), F32),
                pltpu.VMEM((levels, wide), F32),
                pltpu.VMEM((3 * levels, wide), BF16),
                pltpu.VMEM((2 * levels, wide), BF16),
                pltpu.VMEM((16, wide), BF16),
                pltpu.VMEM((16, wide), BF16),
                pltpu.VMEM(pair_weight.shape, F32),
                pltpu.VMEM((6, own + 2 * B), jnp.int32),
                pltpu.VMEM((nb, B), jnp.int32),
                pltpu.VMEM((nb, B), jnp.int32),
                pltpu.VMEM((nb, B), jnp.int32),
                pltpu.VMEM((8, wide), jnp.int32),
                pltpu.VMEM((peers * 4, B), BF16),
                pltpu.VMEM((levels, wide), F32),
                pltpu.VMEM((levels, B), F32),
                pltpu.VMEM((levels, B), F32),
                pltpu.VMEM((nb // 2, 4 * B, 2 * B), BF16),
                pltpu.VMEM((2, 3 * B, B), BF16),
                pltpu.VMEM((1, wide), F32),
                pltpu.VMEM((4 * nb, B), F32),
                pltpu.VMEM((B, B), BF16),
                pltpu.VMEM((peers, 4, B), F32),
                pltpu.VMEM((peers, 4, B), F32),
                pltpu.VMEM((8, wide), F32),
                dma((4,)),
                dma((2,)),
                dma((6,)),
                dma((6,)),
                dma((2,)),
                dma((2,)),
                dma((2,)),
                dma((2,)),
            ],
            compiler_params=pltpu.CompilerParams(
                collective_id=0, has_side_effects=True, vmem_limit_bytes=40 * 2**20
            ),
        )(
            atm_flux.reshape(tracers, atm_cells // B, B),
            ocean_tracer.reshape(levels, own),
            pair_atm,
            pair_count.reshape(1, nb),
            pair_weight,
            neighbors,
            level_count.reshape(nb, B),
            diff_h.reshape(1, levels),
            jnp.pad(diff_v, (0, 1)).reshape(1, levels),
        )
        return ocean[None], surface.reshape(tracers, 1, atm_cells)

    in_specs = (
        P(None, "comp", ("tile", "sub")),
        P("comp", None, ("tile", "sub")),
        P(("tile", "sub"), None),
        P(("tile", "sub")),
        P(("tile", "sub"), None, None, None),
        P(None, ("tile", "sub")),
        P(("tile", "sub")),
        P(),
        P(),
    )
    out_specs = (P("comp", None, ("tile", "sub")), P(None, "comp", ("tile", "sub")))
    return jax.shard_map(local, mesh=mesh, in_specs=in_specs, out_specs=out_specs, check_vma=False)
```

time: 292 us -> 43.9 us (0.15)
  waiting for transfers between devices: 96 us -> 0 us
  local copies, waits for them, and re-layouts: 85.2 us -> 8.75 us
  blocking collectives: 55.3 us -> 0 us
  Pallas kernels: 0 us -> 34.1 us
  starting transfers between devices: 21.8 us -> 0 us
  other arithmetic: 14.2 us -> 0 us
  between operations: 14.4 us -> 0.65 us
  matrix products: 4.01 us -> 0 us
    unnamed x2 -> x0, waiting for transfers between devices: 86.8 us -> none
    gather x19 -> x0, local copies, waits for them, and re-layouts: 73.1 us -> none  [the longest x12 48.4 us: diffuse(): other = jnp.take(values, positions[slot], axis=1)]
    all_gather x1 -> x0, blocking collectives: 55.3 us -> none  [local(): everything = lax.all_gather(atm_flux, ('comp', 'sub'), axis=1, tiled=True)]
    pallas_call x0 -> x1, Pallas kernels: none -> 34.1 us  [local(): pl.pallas_call(functools.partial(kernel, nc, nt, ns, nb, levels), out_sha...]
    ppermute x6 -> x0, starting transfers between devices: 17.5 us -> none  [the longest x3 10.9 us: extended(): lax.ppermute(head, axis, [((i + 1) % count, i) for i in range(ends)])]
    add x2 -> x0, other arithmetic: 9 us -> none  [diffuse(): mixed = centre + diff_horizontal[:, None] * here * total]
    ppermute x6 -> x0, waiting for transfers between devices: 4.8 us -> none  [the longest x3 4.66 us: extended(): lax.ppermute(head, axis, [((i + 1) % count, i) for i in range(ends)])]
    all_to_all x1 -> x0, waiting for transfers between devices: 4.41 us -> none  [local(): lax.all_to_all(summed, 'comp', split_axis=1, concat_axis=0, tiled=True)]
  transfers between devices with their start and end apart: 8 -> 0, of which waited for: 5 -> 0; matrix products, arithmetic and copies ran while one was open for 9% -> 0% of each run, Pallas kernels for 0% -> 0%
where the time goes in v1:
time: 43.9 us; the launch traced here: 43.5 us
  Pallas kernels  34.1 us (78%)
  local copies, waits for them, and re-layouts  8.75 us (20%)
  between operations  0.65 us (1%)
    pallas_call x1, Pallas kernels, local(): pl.pallas_call(functools.partial(kernel, nc, nt, ns, nb, levels), out_sha...  34.1 us
    unnamed x17, local copies, waits for them, and re-layouts  8.09 us

profile of v1, /device:TPU:8, one launch (start us, length us, event | category | flops | bytes accessed | tf_op | source)
XLA Modules:
  0.0 43.5 jit_solution(15914654136656823473)
XLA Ops:
  0.6 0.7 %pad_bitcast_fusion.diff_v = f32[1,80]{1,0:T(1,128)S(1)} fusion(f32[79]{0:T(128)} %param.17), kind=kLoop, calls=%fused_computation | loop fusion | bytes 636 | tf_op jit(solution)/shard_map/reshape | solution.py:361
  1.3 0.8 %copy.11.pair_atm = s32[8,4]{1,0:T(8,128)S(1)} copy(s32[8,4]{0,1:T(4,128)} %param.11) | data formatting | bytes 256 | tf_op args[2]
  2.0 0.0 copy-start
  2.0 1.6 %copy-done = f32[8,4,128,128]{3,2,1,0:T(8,128)S(1)} copy-done((f32[8,4,128,128]{3,2,1,0:T(8,128)S(1)}, f32[8,4,128,128]{3,2,1,0:T(8,128)}, u32[]{:S(2)}) %copy-start) | copy-done | bytes 2097176
  3.6 0.0 copy-start.1
  3.6 1.0 %copy-done.1 = f32[1,80,1024]{2,1,0:T(8,128)S(1)} copy-done((f32[1,80,1024]{2,1,0:T(8,128)S(1)}, f32[1,80,1024]{2,1,0:T(8,128)}, u32[]{:S(2)}) %copy-start.1) | copy-done | bytes 327704
  4.6 0.0 copy-start.2
  4.6 0.8 %copy-done.2 = s32[6,1024]{1,0:T(8,128)S(1)} copy-done((s32[6,1024]{1,0:T(8,128)S(1)}, s32[6,1024]{1,0:T(8,128)}, u32[]{:S(2)}) %copy-start.2) | copy-done | bytes 24600
  5.4 0.0 copy-start.3
  5.4 0.7 %copy-done.3 = f32[4,1,512]{2,1,0:T(1,128)S(1)} copy-done((f32[4,1,512]{2,1,0:T(1,128)S(1)}, f32[4,1,512]{2,1,0:T(1,128)}, u32[]{:S(2)}) %copy-start.3) | copy-done | bytes 8216
  6.1 0.0 copy-start.4
  6.1 0.7 %copy-done.4 = s32[1024]{0:T(1024)S(1)} copy-done((s32[1024]{0:T(1024)S(1)}, s32[1024]{0:T(1024)}, u32[]{:S(2)}) %copy-start.4) | copy-done | bytes 4120
  6.8 0.0 copy-start.5
  6.8 0.7 %copy-done.5 = s32[8]{0:T(128)S(1)} copy-done((s32[8]{0:T(128)S(1)}, s32[8]{0:T(128)}, u32[]{:S(2)}) %copy-start.5) | copy-done | bytes 56
  7.4 0.0 copy-start.6
  7.4 0.7 %copy-done.6 = f32[80]{0:T(128)S(1)} copy-done((f32[80]{0:T(128)S(1)}, f32[80]{0:T(128)}, u32[]{:S(2)}) %copy-start.6) | copy-done | bytes 344
  8.1 34.1 %shard_map.104 = (f32[80,1024]{1,0:T(8,128)S(1)}, f32[4,4,128]{2,1,0:T(4,128)S(1)}) custom-call(f32[4,4,128]{2,1,0:T(4,128)S(1)} %bitcast.11, f32[80,1024]{1,0:T(8,128)S(1)} %bitcast.9, s32[8,4]{1,0:T(8,128)S(1)} %copy.11.pair_atm, s32[1,8]{1,0:T(1,128)S(1)} %bitcast.14, f32[8,4,128,128]{3,2,1,0:T(8,128)S(1)} %copy-done, s32[6,1024]{1,0:T(8,128)S(1)} %copy-done.2, ...), custom_call_target="tpu_custom_call" | custom-call | tf_op jit(solution)/shard_map/pallas_call | solution.py:306
  42.2 0.7 %copy.15 = f32[1,80,1024]{2,1,0:T(8,128)} copy(f32[1,80,1024]{2,1,0:T(8,128)S(1)} %bitcast.10) | data formatting | bytes 655360
  42.9 0.6 %copy.16 = f32[4,1,512]{2,1,0:T(1,128)} copy(f32[4,1,512]{2,1,0:T(1,128)S(1)} %bitcast.12) | data formatting | bytes 16384
Async XLA Ops:
  2.0 1.6 %copy-start = (f32[8,4,128,128]{3,2,1,0:T(8,128)S(1)}, f32[8,4,128,128]{3,2,1,0:T(8,128)}, u32[]{:S(2)}) copy-start(f32[8,4,128,128]{3,2,1,0:T(8,128)} %weight.1) | copy-start | bytes 6291460
  3.6 1.0 %copy-start.1 = (f32[1,80,1024]{2,1,0:T(8,128)S(1)}, f32[1,80,1024]{2,1,0:T(8,128)}, u32[]{:S(2)}) copy-start(f32[1,80,1024]{2,1,0:T(8,128)} %param.10) | copy-start | bytes 983044
  4.6 0.8 %copy-start.2 = (s32[6,1024]{1,0:T(8,128)S(1)}, s32[6,1024]{1,0:T(8,128)}, u32[]{:S(2)}) copy-start(s32[6,1024]{1,0:T(8,128)} %neighbors.1) | copy-start | bytes 73732
  5.4 0.7 %copy-start.3 = (f32[4,1,512]{2,1,0:T(1,128)S(1)}, f32[4,1,512]{2,1,0:T(1,128)}, u32[]{:S(2)}) copy-start(f32[4,1,512]{2,1,0:T(1,128)} %param.9) | copy-start | bytes 24580
  6.1 0.7 %copy-start.4 = (s32[1024]{0:T(1024)S(1)}, s32[1024]{0:T(1024)}, u32[]{:S(2)}) copy-start(s32[1024]{0:T(1024)} %param.15) | copy-start | bytes 12292
  6.8 0.7 %copy-start.5 = (s32[8]{0:T(128)S(1)}, s32[8]{0:T(128)}, u32[]{:S(2)}) copy-start(s32[8]{0:T(128)} %param.12) | copy-start | bytes 100
  7.4 0.7 %copy-start.6 = (f32[80]{0:T(128)S(1)}, f32[80]{0:T(128)}, u32[]{:S(2)}) copy-start(f32[80]{0:T(128)} %param.16) | copy-start | bytes 964

commit v2 on v1

--- a/solution.py
+++ b/solution.py
@@ -32,9 +32,9 @@
 def kernel(
     nc, nt, ns, nb, levels,
     atm, tracer, pair_atm, pair_count, weight, neighbors, depth_own, diff_h, diff_v,
-    ocean, surface,
-    atm_all, v0, v1, x1, x2, xt1, xt2, w, near, depth_l, depth_o, depth_r, depth, table, count,
-    dh, dv, adj, adj_edge, force, contrib, contrib3, parts, arrived, vt1,
+    ocean_hbm, surface,
+    ocean, atm_all, v0, v1, x1, x2, xt1, xt2, w, near, depth_l, depth_o, depth_r, depth, table, count,
+    dh, dv, adj, adj_edge, force, contrib, contrib3, parts, arrived, vt1, goals, counts, dh_row, dv_row,
     sem_load, sem_atm, sem_halo_s, sem_halo_r, sem_force_s, sem_force_r, sem_surf, sem_out,
 ):
     c, t, s = lax.axis_index("comp"), lax.axis_index("tile"), lax.axis_index("sub")
@@ -63,49 +63,6 @@
     lax.fori_loop(1, peers, greet, 0)
     for other in (to_right, to_left):
         pl.semaphore_signal(barrier, inc=1, device_id=other, device_id_type=MESH)
-
-    loads = [
-        pltpu.make_async_copy(neighbors, near.at[:, B : B + own], sem_load.at[0]),
-        pltpu.make_async_copy(depth_own, depth_o, sem_load.at[1]),
-        pltpu.make_async_copy(tracer, v0.at[:, 2 * B : 2 * B + own], sem_load.at[2]),
-        pltpu.make_async_copy(weight, w, sem_load.at[3]),
-    ]
-    for copy in loads:
-        copy.start()
-
-    dh[...] = jnp.broadcast_to(diff_h[...], (B, levels)).T
-    dv[0 : levels, :] = jnp.broadcast_to(diff_v[...], (B, levels)).T
-
-    lane = lax.broadcasted_iota(jnp.int32, (8, B), 1)
-    row = jnp.full((8, B), -1, jnp.int32)
-    for g in range(nb):
-        for k in range(4):
-            goal = jnp.where(k < pair_count[0, g], pair_atm[g, k], -1)
-            row = jnp.where(lane % 32 == g * 4 + k, goal, row)
-    row = jnp.where(lane < 96, row, -1)
-    blocks = peers * 4
-    table[...] = jnp.where(
-        lax.broadcasted_iota(jnp.int32, (blocks, B), 0) == row[0:1], 1.0, 0.0
-    ).astype(BF16)
-
-    start = line * own
-    source = lax.broadcasted_iota(jnp.int32, (B, B), 0)
-
-    def quadrant(target, base):
-        acc = jnp.zeros((B, B), F32)
-        for p in range(6):
-            at = near[p : p + 1, (target - 1) * B : target * B] - (start - 2 * B + base * B)
-            acc = acc + jnp.where(at == source, 1.0, 0.0)
-        return acc.astype(BF16)
-
-    loads[0].wait()
-    for q in range(pairs):
-        a = 2 + 2 * q
-        for i in range(3):
-            adj[q, i * B : (i + 1) * B, 0:B] = quadrant(a, a - 1 + i)
-            adj[q, (i + 1) * B : (i + 2) * B, B : 2 * B] = quadrant(a + 1, a + i)
-        adj[q, 3 * B : 4 * B, 0:B] = jnp.zeros((B, B), BF16)
-        adj[q, 0:B, B : 2 * B] = jnp.zeros((B, B), BF16)
 
     pl.semaphore_wait(barrier, peers - 1 + 2)
 
@@ -136,6 +93,57 @@
         )
         copy.start()
         halo.append(copy)
+
+    loads = [
+        pltpu.make_async_copy(neighbors, near.at[:, B : B + own], sem_load.at[0]),
+        pltpu.make_async_copy(depth_own, depth_o, sem_load.at[1]),
+        pltpu.make_async_copy(tracer, v0.at[:, 2 * B : 2 * B + own], sem_load.at[2]),
+        pltpu.make_async_copy(weight, w, sem_load.at[3]),
+        pltpu.make_async_copy(diff_h, dh_row, sem_load.at[4]),
+        pltpu.make_async_copy(diff_v, dv_row, sem_load.at[5]),
+        pltpu.make_async_copy(pair_atm, goals, sem_load.at[6]),
+        pltpu.make_async_copy(pair_count, counts, sem_load.at[7]),
+    ]
+    for copy in loads:
+        copy.start()
+
+    loads[4].wait()
+    loads[5].wait()
+    dh[...] = jnp.broadcast_to(dh_row[...], (B, levels)).T
+    dv[0 : levels - 1, :] = jnp.broadcast_to(dv_row[...], (B, levels - 1)).T
+    loads[6].wait()
+    loads[7].wait()
+
+    lane = lax.broadcasted_iota(jnp.int32, (8, B), 1)
+    row = jnp.full((8, B), -1, jnp.int32)
+    for g in range(nb):
+        for k in range(4):
+            goal = jnp.where(k < counts[0, g], goals[k, g], -1)
+            row = jnp.where(lane % 32 == g * 4 + k, goal, row)
+    row = jnp.where(lane < 96, row, -1)
+    blocks = peers * 4
+    table[...] = jnp.where(
+        lax.broadcasted_iota(jnp.int32, (blocks, B), 0) == row[0:1], 1.0, 0.0
+    ).astype(BF16)
+
+    start = line * own
+    source = lax.broadcasted_iota(jnp.int32, (B, B), 0)
+
+    def quadrant(target, base):
+        acc = jnp.zeros((B, B), F32)
+        for p in range(6):
+            at = near[p : p + 1, (target - 1) * B : target * B] - (start - 2 * B + base * B)
+            acc = acc + jnp.where(at == source, 1.0, 0.0)
+        return acc.astype(BF16)
+
+    loads[0].wait()
+    for q in range(pairs):
+        a = 2 + 2 * q
+        for i in range(3):
+            adj[q, i * B : (i + 1) * B, 0:B] = quadrant(a, a - 1 + i)
+            adj[q, (i + 1) * B : (i + 2) * B, B : 2 * B] = quadrant(a + 1, a + i)
+        adj[q, 3 * B : 4 * B, 0:B] = jnp.zeros((B, B), BF16)
+        adj[q, 0:B, B : 2 * B] = jnp.zeros((B, B), BF16)
 
     loads[1].wait()
     for g in range(nb):
@@ -203,8 +211,8 @@
     def forcing(g):
         acc = jnp.zeros((B, B), F32)
         for k in range(4):
-            a = pair_atm[g, k]
-            live = jnp.where(k < pair_count[0, g], 1.0, 0.0)
+            a = goals[k, g]
+            live = jnp.where(k < counts[0, g], 1.0, 0.0)
             acc = acc + w[g, k] * (atm_all[a // 4, pl.ds(lax.rem(a, 4), 1), :] * live)
         force[0:1, (2 + g) * B : (3 + g) * B] = jnp.sum(acc.T, axis=0, keepdims=True)
 
@@ -225,10 +233,12 @@
     for g in range(2, nb - 2):
         forcing(g)
 
-    outs = []
     for group in groups:
         lo, n, _ = group
         ocean[:, lo - 2 * B : lo - 2 * B + n] = second(*group)
+
+    out_rest = pltpu.make_async_copy(ocean.at[8:levels], ocean_hbm.at[8:levels], sem_out.at[0])
+    out_rest.start()
 
     for copy in copies:
         copy.wait_recv()
@@ -259,6 +269,9 @@
             for k in range(4):
                 contrib[4 * g + k : 4 * g + k + 1, :] = jnp.sum(w[g, k] * column, axis=0, keepdims=True)
 
+    out_top = pltpu.make_async_copy(ocean.at[0:8], ocean_hbm.at[0:8], sem_out.at[1])
+    out_top.start()
+
     rest = contrib[...]
     for i in range(3):
         part = rest.astype(BF16)
@@ -288,6 +301,8 @@
     pltpu.make_async_copy(parts.at[sent], parts.at[sent], sem_surf.at[0]).wait()
     for copy in halo + copies:
         copy.wait_send()
+    out_rest.wait()
+    out_top.wait()
 
 
 def solution(mesh):
@@ -300,8 +315,7 @@
         wide = own + 4 * B
         peers = nc * ns
         vm = pl.BlockSpec(memory_space=pltpu.VMEM)
-        sm = pl.BlockSpec(memory_space=pltpu.SMEM)
-        anywhere = pl.BlockSpec(memory_space=pl.ANY)
+        hbm = pl.BlockSpec(memory_space=pltpu.HBM)
         dma = pltpu.SemaphoreType.DMA
         ocean, surface = pl.pallas_call(
             functools.partial(kernel, nc, nt, ns, nb, levels),
@@ -309,9 +323,10 @@
                 jax.ShapeDtypeStruct((levels, own), F32),
                 jax.ShapeDtypeStruct((tracers, atm_cells // B, B), F32),
             ),
-            in_specs=[anywhere, anywhere, sm, sm, anywhere, anywhere, anywhere, vm, vm],
-            out_specs=(vm, vm),
+            in_specs=[hbm] * 9,
+            out_specs=(hbm, vm),
             scratch_shapes=[
+                pltpu.VMEM((levels, own), F32),
                 pltpu.VMEM((peers, 4, B), F32),
                 pltpu.VMEM((levels, wide), F32),
                 pltpu.VMEM((levels, wide), F32),
@@ -337,28 +352,32 @@
                 pltpu.VMEM((peers, 4, B), F32),
                 pltpu.VMEM((peers, 4, B), F32),
                 pltpu.VMEM((8, wide), F32),
-                dma((4,)),
+                pltpu.SMEM((4, nb), jnp.int32),
+                pltpu.SMEM((1, nb), jnp.int32),
+                pltpu.VMEM((1, levels), F32),
+                pltpu.VMEM((1, levels - 1), F32),
+                dma((8,)),
                 dma((2,)),
                 dma((6,)),
                 dma((6,)),
                 dma((2,)),
                 dma((2,)),
                 dma((2,)),
-                dma((2,)),
+                    dma((2,)),
             ],
             compiler_params=pltpu.CompilerParams(
-                collective_id=0, has_side_effects=True, vmem_limit_bytes=40 * 2**20
+                collective_id=0, has_side_effects=True, vmem_limit_bytes=63 * 2**20
             ),
         )(
             atm_flux.reshape(tracers, atm_cells // B, B),
             ocean_tracer.reshape(levels, own),
-            pair_atm,
+            pair_atm.T,
             pair_count.reshape(1, nb),
             pair_weight,
             neighbors,
             level_count.reshape(nb, B),
             diff_h.reshape(1, levels),
-            jnp.pad(diff_v, (0, 1)).reshape(1, levels),
+            diff_v.reshape(1, levels - 1),
         )
         return ocean[None], surface.reshape(tracers, 1, atm_cells)
 

time: 43.9 us -> 38.3 us (0.87)
  local copies, waits for them, and re-layouts: 8.75 us -> 3.02 us
    unnamed x17 -> x2, local copies, waits for them, and re-layouts: 8.09 us -> 3.02 us
    reshape x1 -> x0, local copies, waits for them, and re-layouts: 0.66 us -> none  [local(): jnp.pad(diff_v, (0, 1)).reshape(1, levels)]
where the time goes in v2:
time: 38.3 us; the launch traced here: 38 us
  Pallas kernels  34.4 us (90%)
  local copies, waits for them, and re-layouts  3.02 us (8%)
  between operations  0.64 us (2%)
    pallas_call x1, Pallas kernels, local(): pl.pallas_call(functools.partial(kernel, nc, nt, ns, nb, levels), out_sha...  34.4 us
    unnamed x2, local copies, waits for them, and re-layouts  3.02 us

profile of v2, /device:TPU:8, one launch (start us, length us, event | category | flops | bytes accessed | tf_op | source)
XLA Modules:
  0.0 38.0 jit_solution(9699372876180369266)
XLA Ops:
  0.6 34.4 %shard_map.104 = (f32[80,1024]{1,0:T(8,128)}, f32[4,4,128]{2,1,0:T(4,128)}) custom-call(f32[4,4,128]{2,1,0:T(4,128)} %bitcast.11, f32[80,1024]{1,0:T(8,128)} %bitcast.10, s32[4,8]{1,0:T(4,128)} %bitcast.14, s32[1,8]{1,0:T(1,128)} %bitcast.15, f32[8,4,128,128]{3,2,1,0:T(8,128)} %weight.1, s32[6,1024]{1,0:T(8,128)} %neighbors.1, s32[8,128]{1,0:T(8,128)} %bitcast.13, ...), custom_call_target="tpu_custom_call" | custom-call | tf_op jit(solution)/shard_map/pallas_call | solution.py:320
  35.0 1.7 %copy.14 = f32[1,80,1024]{2,1,0:T(8,128)} copy(f32[1,80,1024]{2,1,0:T(8,128)} %bitcast.9) | data formatting | bytes 655360
  36.7 1.3 %copy.15 = f32[4,1,512]{2,1,0:T(1,128)} copy(f32[4,1,512]{2,1,0:T(1,128)} %bitcast.12) | data formatting | bytes 16384

commit v3 on v2

--- a/solution.py
+++ b/solution.py
@@ -32,10 +32,10 @@
 def kernel(
     nc, nt, ns, nb, levels,
     atm, tracer, pair_atm, pair_count, weight, neighbors, depth_own, diff_h, diff_v,
-    ocean_hbm, surface,
-    ocean, atm_all, v0, v1, x1, x2, xt1, xt2, w, near, depth_l, depth_o, depth_r, depth, table, count,
+    ocean, surface,
+    atm_all, v0, v1, x1, x2, xt1, xt2, w, near, depth_l, depth_o, depth_r, depth, table, count,
     dh, dv, adj, adj_edge, force, contrib, contrib3, parts, arrived, vt1, goals, counts, dh_row, dv_row,
-    sem_load, sem_atm, sem_halo_s, sem_halo_r, sem_force_s, sem_force_r, sem_surf, sem_out,
+    sem_load, sem_atm, sem_halo_s, sem_halo_r, sem_force_s, sem_force_r, sem_surf, sem_bulk, ready,
 ):
     c, t, s = lax.axis_index("comp"), lax.axis_index("tile"), lax.axis_index("sub")
     own = nb * B
@@ -53,6 +53,13 @@
         ps = lax.rem(s + lax.rem(d, ns), ns)
         return pc, ps
 
+    first_slot = slot == 0
+    has_left, has_right = line > 0, line < nt * ns - 1
+    leads = jnp.logical_and(s == 0, has_left)
+    trails = jnp.logical_and(s == ns - 1, has_right)
+    beside = jnp.logical_and(c == 0, s == 1)
+    one = jnp.int32(1)
+    zero = jnp.int32(0)
     barrier = pltpu.get_barrier_semaphore()
 
     def greet(d, carry):
@@ -60,22 +67,52 @@
         pl.semaphore_signal(barrier, inc=1, device_id=(pc, t, ps), device_id_type=MESH)
         return carry
 
-    lax.fori_loop(1, peers, greet, 0)
-    for other in (to_right, to_left):
-        pl.semaphore_signal(barrier, inc=1, device_id=other, device_id_type=MESH)
-
-    pl.semaphore_wait(barrier, peers - 1 + 2)
+    @pl.when(jnp.logical_not(first_slot))
+    def _():
+        lax.fori_loop(1, peers, greet, 0)
+
+    @pl.when(trails)
+    def _():
+        pl.semaphore_signal(barrier, inc=1, device_id=to_right, device_id_type=MESH)
+
+    pl.semaphore_wait(
+        barrier,
+        peers - 2 + jnp.where(first_slot, one, zero) + jnp.where(leads, one, zero),
+    )
+
+    def tell(d, carry):
+        pc, ps = peer(d)
+        pl.semaphore_signal(ready.at[0], inc=1, device_id=(pc, t, ps), device_id_type=MESH)
+        return carry
+
+    @pl.when(first_slot)
+    def _():
+        tell(1, 0)
+
+    @pl.when(leads)
+    def _():
+        pl.semaphore_signal(ready.at[1], inc=1, device_id=to_left, device_id_type=MESH)
+
+    landing = sem_atm.at[jnp.where(first_slot, 2 * one, one)]
 
     def send_atm(d, carry):
         pc, ps = peer(d)
-        pltpu.make_async_remote_copy(
-            src_ref=atm.at[pc], dst_ref=atm_all.at[slot], send_sem=sem_atm.at[0], recv_sem=sem_atm.at[1],
-            device_id=(pc, t, ps), device_id_type=MESH,
-        ).start()
+
+        @pl.when(pc * ns + ps != 0)
+        def _():
+            pltpu.make_async_remote_copy(
+                src_ref=atm.at[pc], dst_ref=atm_all.at[slot], send_sem=sem_atm.at[0], recv_sem=landing,
+                device_id=(pc, t, ps), device_id_type=MESH,
+            ).start()
+
         return carry
 
     lax.fori_loop(1, peers, send_atm, 0)
-    pltpu.make_async_copy(atm.at[c], atm_all.at[slot], sem_atm.at[1]).start()
+    pltpu.make_async_copy(atm.at[c], atm_all.at[slot], landing).start()
+
+    @pl.when(first_slot)
+    def _():
+        lax.fori_loop(2, peers, tell, 0)
 
     halo = []
     plan = [
@@ -87,12 +124,36 @@
         (tracer.at[:, 0 : 2 * B], v0.at[:, 2 * B + own : wide], to_left),
     ]
     for i, (src, dst, other) in enumerate(plan):
-        copy = pltpu.make_async_remote_copy(
-            src_ref=src, dst_ref=dst, send_sem=sem_halo_s.at[i], recv_sem=sem_halo_r.at[i],
-            device_id=other, device_id_type=MESH,
+        halo.append(
+            pltpu.make_async_remote_copy(
+                src_ref=src, dst_ref=dst, send_sem=sem_halo_s.at[i], recv_sem=sem_halo_r.at[i],
+                device_id=other, device_id_type=MESH,
+            )
         )
-        copy.start()
-        halo.append(copy)
+
+    @pl.when(s < ns - 1)
+    def _():
+        for i in (0, 2, 4):
+            halo[i].start()
+
+    @pl.when(jnp.logical_and(has_left, jnp.logical_not(beside)))
+    def _():
+        for i in (1, 3, 5):
+            halo[i].start()
+
+    @pl.when(jnp.logical_not(has_left))
+    def _():
+        depth_l[...] = jnp.zeros_like(depth_l)
+        near[:, 0:B] = jnp.zeros((6, B), jnp.int32)
+        v0[:, 0 : 2 * B] = jnp.zeros((levels, 2 * B), F32)
+        force[:, 0 : 2 * B] = jnp.zeros((1, 2 * B), F32)
+
+    @pl.when(jnp.logical_not(has_right))
+    def _():
+        depth_r[...] = jnp.zeros_like(depth_r)
+        near[:, B + own : 2 * B + own] = jnp.zeros((6, B), jnp.int32)
+        v0[:, 2 * B + own : wide] = jnp.zeros((levels, 2 * B), F32)
+        force[:, 2 * B + own : wide] = jnp.zeros((1, 2 * B), F32)
 
     loads = [
         pltpu.make_async_copy(neighbors, near.at[:, B : B + own], sem_load.at[0]),
@@ -188,25 +249,33 @@
         prepare_first(2 * B + 2 * B * q, 2 * B)
     for group in groups[1:-1]:
         first(*group)
-    for i in range(4):
-        halo[i].wait_recv()
-    for i in range(2):
-        depth[:, i * B : (i + 1) * B] = jnp.broadcast_to(depth_l[nb - 2 + i : nb - 1 + i, :], (8, B))
-        depth[:, (2 + nb + i) * B : (3 + nb + i) * B] = jnp.broadcast_to(depth_r[i : i + 1, :], (8, B))
-        target = 1 + i * (nb + 1)
-        for j in range(3):
-            adj_edge[i, j * B : (j + 1) * B, :] = quadrant(target, target - 1 + j)
-    for i in range(4, 6):
-        halo[i].wait_recv()
-    prepare_first(0, 2 * B)
-    prepare_first(2 * B + own, 2 * B)
-    first(*groups[0])
-    first(*groups[-1])
-    for edge in edges:
-        first(*edge)
+    rest = atm_all.at[pl.ds(1, peers - 1)]
+    bulk = pltpu.make_async_remote_copy(
+        src_ref=rest, dst_ref=rest, send_sem=sem_bulk, recv_sem=sem_atm.at[1],
+        device_id=(c, t, lax.rem(s + ns - 1, ns)), device_id_type=MESH,
+    )
+
+    @pl.when(trails)
+    def _():
+        pl.semaphore_wait(ready.at[1], 1)
+        for i in (0, 2, 4):
+            halo[i].start()
+
+    @pl.when(beside)
+    def _():
+        pl.semaphore_wait(ready.at[0], 1)
+        for i in (1, 3, 5):
+            halo[i].start()
+
+    pltpu.make_async_copy(rest, rest, sem_atm.at[1]).wait()
+
+    @pl.when(beside)
+    def _():
+        bulk.start()
 
     loads[3].wait()
-    pltpu.make_async_copy(atm_all, atm_all, sem_atm.at[1]).wait()
+    root = atm_all.at[pl.ds(0, 1)]
+    pltpu.make_async_copy(root, root, sem_atm.at[2]).wait()
 
     def forcing(g):
         acc = jnp.zeros((B, B), F32)
@@ -216,32 +285,50 @@
             acc = acc + w[g, k] * (atm_all[a // 4, pl.ds(lax.rem(a, 4), 1), :] * live)
         force[0:1, (2 + g) * B : (3 + g) * B] = jnp.sum(acc.T, axis=0, keepdims=True)
 
-    def send_force(i, lo, goal, other):
+    def send_force(i, lo, goal, other, there):
         copy = pltpu.make_async_remote_copy(
             src_ref=force.at[:, lo : lo + 2 * B], dst_ref=force.at[:, goal : goal + 2 * B],
             send_sem=sem_force_s.at[i], recv_sem=sem_force_r.at[i], device_id=other, device_id_type=MESH,
         )
-        copy.start()
+        pl.when(there)(copy.start)
         return copy
 
     for g in (nb - 2, nb - 1):
         forcing(g)
-    copies = [send_force(0, own, 0, to_right)]
+    copies = [send_force(0, own, 0, to_right, has_right)]
     for g in (0, 1):
         forcing(g)
-    copies.append(send_force(1, 2 * B, 2 * B + own, to_left))
+    copies.append(send_force(1, 2 * B, 2 * B + own, to_left, has_left))
     for g in range(2, nb - 2):
         forcing(g)
+
+    def of_sides(to_left_too, to_right_too):
+        pl.when(has_left)(to_left_too)
+        pl.when(has_right)(to_right_too)
+
+    of_sides(
+        lambda: [halo[i].wait_recv() for i in (0, 2)] and None,
+        lambda: [halo[i].wait_recv() for i in (1, 3)] and None,
+    )
+    for i in range(2):
+        depth[:, i * B : (i + 1) * B] = jnp.broadcast_to(depth_l[nb - 2 + i : nb - 1 + i, :], (8, B))
+        depth[:, (2 + nb + i) * B : (3 + nb + i) * B] = jnp.broadcast_to(depth_r[i : i + 1, :], (8, B))
+        target = 1 + i * (nb + 1)
+        for j in range(3):
+            adj_edge[i, j * B : (j + 1) * B, :] = quadrant(target, target - 1 + j)
+    of_sides(halo[4].wait_recv, halo[5].wait_recv)
+    prepare_first(0, 2 * B)
+    prepare_first(2 * B + own, 2 * B)
+    first(*groups[0])
+    first(*groups[-1])
+    for edge in edges:
+        first(*edge)
 
     for group in groups:
         lo, n, _ = group
         ocean[:, lo - 2 * B : lo - 2 * B + n] = second(*group)
 
-    out_rest = pltpu.make_async_copy(ocean.at[8:levels], ocean_hbm.at[8:levels], sem_out.at[0])
-    out_rest.start()
-
-    for copy in copies:
-        copy.wait_recv()
+    of_sides(copies[0].wait_recv, copies[1].wait_recv)
 
     k8 = lax.broadcasted_iota(jnp.int32, (8, wide), 0)
     top = v0[0:8, :] + jnp.where(k8 == 0, jnp.broadcast_to(force[...], (8, wide)), 0.0)
@@ -269,9 +356,6 @@
             for k in range(4):
                 contrib[4 * g + k : 4 * g + k + 1, :] = jnp.sum(w[g, k] * column, axis=0, keepdims=True)
 
-    out_top = pltpu.make_async_copy(ocean.at[0:8], ocean_hbm.at[0:8], sem_out.at[1])
-    out_top.start()
-
     rest = contrib[...]
     for i in range(3):
         part = rest.astype(BF16)
@@ -290,6 +374,10 @@
         ).start()
         return carry
 
+    @pl.when(jnp.logical_not(jnp.logical_or(first_slot, beside)))
+    def _():
+        pl.semaphore_wait(ready.at[0], 1)
+
     lax.fori_loop(1, peers, send_part, 0)
     pltpu.make_async_copy(parts.at[slot], arrived.at[slot], sem_surf.at[1]).start()
     pltpu.make_async_copy(arrived, arrived, sem_surf.at[1]).wait()
@@ -297,12 +385,25 @@
         surface[i] = jnp.sum(arrived[i * ns : (i + 1) * ns], axis=0)
 
     sent = pl.ds(0, peers - 1)
-    pltpu.make_async_copy(atm_all.at[sent], atm_all.at[sent], sem_atm.at[0]).wait()
+    fewer = pl.ds(0, peers - 2)
+
+    @pl.when(first_slot)
+    def _():
+        pltpu.make_async_copy(atm_all.at[sent], atm_all.at[sent], sem_atm.at[0]).wait()
+
+    @pl.when(jnp.logical_not(first_slot))
+    def _():
+        pltpu.make_async_copy(atm_all.at[fewer], atm_all.at[fewer], sem_atm.at[0]).wait()
+
+    @pl.when(beside)
+    def _():
+        bulk.wait_send()
+
     pltpu.make_async_copy(parts.at[sent], parts.at[sent], sem_surf.at[0]).wait()
-    for copy in halo + copies:
-        copy.wait_send()
-    out_rest.wait()
-    out_top.wait()
+    of_sides(
+        lambda: [copy.wait_send() for copy in (halo[1], halo[3], halo[5], copies[1])] and None,
+        lambda: [copy.wait_send() for copy in (halo[0], halo[2], halo[4], copies[0])] and None,
+    )
 
 
 def solution(mesh):
@@ -320,13 +421,12 @@
         ocean, surface = pl.pallas_call(
             functools.partial(kernel, nc, nt, ns, nb, levels),
             out_shape=(
-                jax.ShapeDtypeStruct((levels, own), F32),
-                jax.ShapeDtypeStruct((tracers, atm_cells // B, B), F32),
+                pltpu.VMEM((levels, own), F32),
+                pltpu.VMEM((tracers, atm_cells // B, B), F32),
             ),
             in_specs=[hbm] * 9,
-            out_specs=(hbm, vm),
+            out_specs=(vm, vm),
             scratch_shapes=[
-                pltpu.VMEM((levels, own), F32),
                 pltpu.VMEM((peers, 4, B), F32),
                 pltpu.VMEM((levels, wide), F32),
                 pltpu.VMEM((levels, wide), F32),
@@ -357,18 +457,19 @@
                 pltpu.VMEM((1, levels), F32),
                 pltpu.VMEM((1, levels - 1), F32),
                 dma((8,)),
-                dma((2,)),
+                dma((3,)),
                 dma((6,)),
                 dma((6,)),
                 dma((2,)),
                 dma((2,)),
                 dma((2,)),
-                    dma((2,)),
+                    dma,
+                pltpu.SemaphoreType.REGULAR((2,)),
             ],
             compiler_params=pltpu.CompilerParams(
-                collective_id=0, has_side_effects=True, vmem_limit_bytes=63 * 2**20
+                collective_id=0, has_side_effects=True, vmem_limit_bytes=40 * 2**20
             ),
-        )(
+        )(*(pltpu.with_memory_space_constraint(x, pltpu.HBM) for x in (
             atm_flux.reshape(tracers, atm_cells // B, B),
             ocean_tracer.reshape(levels, own),
             pair_atm.T,
@@ -378,7 +479,7 @@
             level_count.reshape(nb, B),
             diff_h.reshape(1, levels),
             diff_v.reshape(1, levels - 1),
-        )
+        )))
         return ocean[None], surface.reshape(tracers, 1, atm_cells)
 
     in_specs = (

time: 38.3 us -> 30.1 us (0.79)
  the two profiles are of different devices: /device:TPU:8 before, /device:TPU:199 now
where the time goes in v3:
time: 30.1 us; the launch traced here: 30 us
  Pallas kernels  28 us (93%)
  local copies, waits for them, and re-layouts  1.32 us (4%)
  between operations  0.64 us (2%)
    pallas_call x1, Pallas kernels, local(): pl.pallas_call(functools.partial(kernel, nc, nt, ns, nb, levels), out_sha...  28 us
    unnamed x2, local copies, waits for them, and re-layouts  1.32 us

profile of v3, /device:TPU:199, one launch (start us, length us, event | category | flops | bytes accessed | tf_op | source)
XLA Modules:
  0.0 30.0 jit_solution(16832250566944819472)
XLA Ops:
  0.6 28.0 %shard_map.104 = (f32[80,1024]{1,0:T(8,128)S(1)}, f32[4,4,128]{2,1,0:T(4,128)S(1)}) custom-call(f32[4,4,128]{2,1,0:T(4,128)} %bitcast.12, f32[80,1024]{1,0:T(8,128)} %bitcast.11, s32[4,8]{1,0:T(4,128)} %bitcast.14, s32[1,8]{1,0:T(1,128)} %bitcast.15, f32[8,4,128,128]{3,2,1,0:T(8,128)} %weight.1, s32[6,1024]{1,0:T(8,128)} %neighbors.1, s32[8,128]{1,0:T(8,128)} %bitcast.13, ...), custom_call_target="tpu_custom_call" | custom-call | tf_op jit(solution)/shard_map/pallas_call | solution.py:421
  28.7 0.7 %copy.14 = f32[1,80,1024]{2,1,0:T(8,128)} copy(f32[1,80,1024]{2,1,0:T(8,128)S(1)} %bitcast.9) | data formatting | bytes 655360
  29.4 0.6 %copy.15 = f32[4,1,512]{2,1,0:T(1,128)} copy(f32[4,1,512]{2,1,0:T(1,128)S(1)} %bitcast.10) | data formatting | bytes 16384

commit v4 on v3

--- a/solution.py
+++ b/solution.py
@@ -34,7 +34,7 @@
     atm, tracer, pair_atm, pair_count, weight, neighbors, depth_own, diff_h, diff_v,
     ocean, surface,
     atm_all, v0, v1, x1, x2, xt1, xt2, w, near, depth_l, depth_o, depth_r, depth, table, count,
-    dh, dv, adj, adj_edge, force, contrib, contrib3, parts, arrived, vt1, goals, counts, dh_row, dv_row,
+    dh, dv, adj, adj_edge, force, contrib, contrib3, parts, arrived, vt0, vt1, vt2, goals, counts, dh_row, dv_row,
     sem_load, sem_atm, sem_halo_s, sem_halo_r, sem_force_s, sem_force_r, sem_surf, sem_bulk, ready,
 ):
     c, t, s = lax.axis_index("comp"), lax.axis_index("tile"), lax.axis_index("sub")
@@ -53,23 +53,32 @@
         ps = lax.rem(s + lax.rem(d, ns), ns)
         return pc, ps
 
-    first_slot = slot == 0
+    def each_peer(body):
+        for dc in sorted(range(nc), key=lambda d: -min(d, nc - d)):
+            def at(k, carry, dc=dc):
+                off = (k + 1) // 2
+                ds = lax.rem(ns // 2 + off * (1 - 2 * lax.rem(k, 2)) + ns, ns)
+                pc, ps = lax.rem(c + dc, nc), lax.rem(s + ds, ns)
+                body(pc, ps)
+                return carry
+
+            lax.fori_loop(0, ns - 1 if dc == 0 else ns, at, 0, unroll=True)
+
+    first_slot = jnp.logical_and(slot == 0, t == 0)
     has_left, has_right = line > 0, line < nt * ns - 1
     leads = jnp.logical_and(s == 0, has_left)
     trails = jnp.logical_and(s == ns - 1, has_right)
-    beside = jnp.logical_and(c == 0, s == 1)
+    beside = jnp.logical_and(jnp.logical_and(c == 0, s == 1), t == 0)
     one = jnp.int32(1)
     zero = jnp.int32(0)
     barrier = pltpu.get_barrier_semaphore()
 
-    def greet(d, carry):
-        pc, ps = peer(d)
+    def greet(pc, ps):
         pl.semaphore_signal(barrier, inc=1, device_id=(pc, t, ps), device_id_type=MESH)
-        return carry
 
     @pl.when(jnp.logical_not(first_slot))
     def _():
-        lax.fori_loop(1, peers, greet, 0)
+        each_peer(greet)
 
     @pl.when(trails)
     def _():
@@ -77,7 +86,7 @@
 
     pl.semaphore_wait(
         barrier,
-        peers - 2 + jnp.where(first_slot, one, zero) + jnp.where(leads, one, zero),
+        peers - 1 - jnp.where(jnp.logical_and(t == 0, slot > 0), one, zero) + jnp.where(leads, one, zero),
     )
 
     def tell(d, carry):
@@ -93,21 +102,17 @@
     def _():
         pl.semaphore_signal(ready.at[1], inc=1, device_id=to_left, device_id_type=MESH)
 
-    landing = sem_atm.at[jnp.where(first_slot, 2 * one, one)]
-
-    def send_atm(d, carry):
-        pc, ps = peer(d)
-
-        @pl.when(pc * ns + ps != 0)
+    landing = sem_atm.at[jnp.where(slot == 0, 2 * one, one)]
+
+    def send_atm(pc, ps):
+        @pl.when(jnp.logical_or(t > 0, pc * ns + ps != 0))
         def _():
             pltpu.make_async_remote_copy(
                 src_ref=atm.at[pc], dst_ref=atm_all.at[slot], send_sem=sem_atm.at[0], recv_sem=landing,
                 device_id=(pc, t, ps), device_id_type=MESH,
             ).start()
 
-        return carry
-
-    lax.fori_loop(1, peers, send_atm, 0)
+    each_peer(send_atm)
     pltpu.make_async_copy(atm.at[c], atm_all.at[slot], landing).start()
 
     @pl.when(first_slot)
@@ -301,6 +306,43 @@
     copies.append(send_force(1, 2 * B, 2 * B + own, to_left, has_left))
     for g in range(2, nb - 2):
         forcing(g)
+
+    def top_fill(lo, n):
+        k = lax.broadcasted_iota(jnp.int32, (8, n), 0)
+        new = v0[0:8, lo : lo + n] + jnp.where(k == 0, jnp.broadcast_to(force[:, lo : lo + n], (8, n)), 0.0)
+        vt0[:, lo : lo + n] = new
+        prepare(new, xt1, lo, n)
+
+    def top_step(centre, store, lo, n, matrix):
+        r = jnp.dot(store[:, lo - B : lo + n + B], matrix[...], preferred_element_type=F32)
+        return relax(
+            centre, r[0:8] + r[8:16], count[0:8, lo : lo + n], depth[0:1, lo : lo + n],
+            jnp.concatenate([dh[0:8, :]] * (n // B), 1), jnp.concatenate([dv[0:8, :]] * (n // B), 1),
+        )
+
+    def top_first(lo, n, matrix):
+        new = top_step(vt0[:, lo : lo + n], xt1, lo, n, matrix)
+        vt1[:, lo : lo + n] = new
+        prepare(new, xt2, lo, n)
+
+    def top_second(lo, n, matrix):
+        new = top_step(vt1[:, lo : lo + n], xt2, lo, n, matrix)
+        vt2[:, lo : lo + n] = new
+        for half in range(n // B):
+            g = (lo - 2 * B) // B + half
+            column = jnp.broadcast_to(new[0:1, half * B : (half + 1) * B], (B, B)).T
+            for k in range(4):
+                contrib[4 * g + k : 4 * g + k + 1, :] = jnp.sum(w[g, k] * column, axis=0, keepdims=True)
+
+    top_fill(2 * B, own)
+    for group in groups[1:-1]:
+        top_first(*group)
+    for lo, matrix in ((3 * B, adj.at[0, B : 4 * B, B : 2 * B]), (own, adj.at[pairs - 1, 0 : 3 * B, 0:B])):
+        live = x1[2 * levels : 2 * levels + 16, lo - B : lo + 2 * B]
+        count[0:8, lo : lo + B] = jnp.dot(live, matrix[...], preferred_element_type=F32)[0:8]
+        top_first(lo, B, matrix)
+    for group in groups[1:-1]:
+        top_second(*group)
 
     def of_sides(to_left_too, to_right_too):
         pl.when(has_left)(to_left_too)
@@ -324,37 +366,15 @@
     for edge in edges:
         first(*edge)
 
-    for group in groups:
-        lo, n, _ = group
-        ocean[:, lo - 2 * B : lo - 2 * B + n] = second(*group)
-
     of_sides(copies[0].wait_recv, copies[1].wait_recv)
-
-    k8 = lax.broadcasted_iota(jnp.int32, (8, wide), 0)
-    top = v0[0:8, :] + jnp.where(k8 == 0, jnp.broadcast_to(force[...], (8, wide)), 0.0)
-    prepare(top, xt1, 0, wide)
-
-    def top_step(centre, store, lo, n, matrix):
-        r = jnp.dot(store[:, lo - B : lo + n + B], matrix[...], preferred_element_type=F32)
-        return relax(
-            centre, r[0:8] + r[8:16], count[0:8, lo : lo + n], depth[0:1, lo : lo + n],
-            jnp.concatenate([dh[0:8, :]] * (n // B), 1), jnp.concatenate([dv[0:8, :]] * (n // B), 1),
-        )
-
-    for lo, n, matrix in groups + edges:
-        new = top_step(top[:, lo : lo + n], xt1, lo, n, matrix)
-        vt1[:, lo : lo + n] = new
-        prepare(new, xt2, lo, n)
-    for lo, n, matrix in groups:
-        new = top_step(vt1[:, lo : lo + n], xt2, lo, n, matrix)
-        k = lax.broadcasted_iota(jnp.int32, (8, n), 0)
-        here = slice(lo - 2 * B, lo - 2 * B + n)
-        ocean[0:8, here] = jnp.where(k < 3, new, ocean[0:8, here])
-        for half in range(n // B):
-            g = (lo - 2 * B) // B + half
-            column = jnp.broadcast_to(new[0:1, half * B : (half + 1) * B], (B, B)).T
-            for k in range(4):
-                contrib[4 * g + k : 4 * g + k + 1, :] = jnp.sum(w[g, k] * column, axis=0, keepdims=True)
+    for lo in (0, 2 * B + own):
+        top_fill(lo, 2 * B)
+    for lo, n, matrix in edges:
+        top_first(lo, n, matrix)
+    top_first(2 * B, B, adj.at[0, 0 : 3 * B, 0:B])
+    top_first(own + B, B, adj.at[pairs - 1, B : 4 * B, B : 2 * B])
+    top_second(*groups[0])
+    top_second(*groups[-1])
 
     rest = contrib[...]
     for i in range(3):
@@ -366,20 +386,26 @@
     for i in range(peers):
         parts[i] = summed[4 * i : 4 * (i + 1)]
 
-    def send_part(d, carry):
-        pc, ps = peer(d)
+    def send_part(pc, ps):
         pltpu.make_async_remote_copy(
             src_ref=parts.at[pc * ns + ps], dst_ref=arrived.at[slot], send_sem=sem_surf.at[0], recv_sem=sem_surf.at[1],
             device_id=(pc, t, ps), device_id_type=MESH,
         ).start()
-        return carry
-
-    @pl.when(jnp.logical_not(jnp.logical_or(first_slot, beside)))
+
+    @pl.when(jnp.logical_and(t == 0, jnp.logical_not(jnp.logical_or(first_slot, beside))))
     def _():
         pl.semaphore_wait(ready.at[0], 1)
 
-    lax.fori_loop(1, peers, send_part, 0)
+    each_peer(send_part)
     pltpu.make_async_copy(parts.at[slot], arrived.at[slot], sem_surf.at[1]).start()
+
+    for lo, n, matrix in groups:
+        here = slice(lo - 2 * B, lo - 2 * B + n)
+        new = second(lo, n, matrix)
+        k = lax.broadcasted_iota(jnp.int32, (8, n), 0)
+        ocean[8:levels, here] = new[8:levels]
+        ocean[0:8, here] = jnp.where(k < 3, vt2[:, lo : lo + n], new[0:8])
+
     pltpu.make_async_copy(arrived, arrived, sem_surf.at[1]).wait()
     for i in range(nc):
         surface[i] = jnp.sum(arrived[i * ns : (i + 1) * ns], axis=0)
@@ -387,11 +413,13 @@
     sent = pl.ds(0, peers - 1)
     fewer = pl.ds(0, peers - 2)
 
-    @pl.when(first_slot)
+    skips = jnp.logical_and(t == 0, slot > 0)
+
+    @pl.when(jnp.logical_not(skips))
     def _():
         pltpu.make_async_copy(atm_all.at[sent], atm_all.at[sent], sem_atm.at[0]).wait()
 
-    @pl.when(jnp.logical_not(first_slot))
+    @pl.when(skips)
     def _():
         pltpu.make_async_copy(atm_all.at[fewer], atm_all.at[fewer], sem_atm.at[0]).wait()
 
@@ -452,6 +480,8 @@
                 pltpu.VMEM((peers, 4, B), F32),
                 pltpu.VMEM((peers, 4, B), F32),
                 pltpu.VMEM((8, wide), F32),
+                pltpu.VMEM((8, wide), F32),
+                pltpu.VMEM((8, wide), F32),
                 pltpu.SMEM((4, nb), jnp.int32),
                 pltpu.SMEM((1, nb), jnp.int32),
                 pltpu.VMEM((1, levels), F32),

time: 30.1 us -> 26.9 us (0.89)
  the two profiles are of different devices: /device:TPU:199 before, /device:TPU:8 now
where the time goes in v4:
time: 26.9 us; the launch traced here: 26.7 us
  Pallas kernels  24.7 us (92%)
  local copies, waits for them, and re-layouts  1.32 us (5%)
  between operations  0.64 us (2%)
    pallas_call x1, Pallas kernels, local(): pl.pallas_call(functools.partial(kernel, nc, nt, ns, nb, levels), out_sha...  24.7 us
    unnamed x2, local copies, waits for them, and re-layouts  1.32 us

profile of v4, /device:TPU:8, one launch (start us, length us, event | category | flops | bytes accessed | tf_op | source)
XLA Modules:
  0.0 26.7 jit_solution(12444054911564566495)
XLA Ops:
  0.6 24.7 %shard_map.104 = (f32[80,1024]{1,0:T(8,128)S(1)}, f32[4,4,128]{2,1,0:T(4,128)S(1)}) custom-call(f32[4,4,128]{2,1,0:T(4,128)} %bitcast.12, f32[80,1024]{1,0:T(8,128)} %bitcast.11, s32[4,8]{1,0:T(4,128)} %bitcast.14, s32[1,8]{1,0:T(1,128)} %bitcast.15, f32[8,4,128,128]{3,2,1,0:T(8,128)} %weight.1, s32[6,1024]{1,0:T(8,128)} %neighbors.1, s32[8,128]{1,0:T(8,128)} %bitcast.13, ...), custom_call_target="tpu_custom_call" | custom-call | tf_op jit(solution)/shard_map/pallas_call | solution.py:449
  25.4 0.7 %copy.14 = f32[1,80,1024]{2,1,0:T(8,128)} copy(f32[1,80,1024]{2,1,0:T(8,128)S(1)} %bitcast.9) | data formatting | bytes 655360
  26.1 0.6 %copy.15 = f32[4,1,512]{2,1,0:T(1,128)} copy(f32[4,1,512]{2,1,0:T(1,128)S(1)} %bitcast.10) | data formatting | bytes 16384

commit v5 on v4

--- a/solution.py
+++ b/solution.py
@@ -432,6 +432,14 @@
         lambda: [copy.wait_send() for copy in (halo[1], halo[3], halo[5], copies[1])] and None,
         lambda: [copy.wait_send() for copy in (halo[0], halo[2], halo[4], copies[0])] and None,
     )
+
+
+def store(ocean, surface, ocean_out, surface_out, sem):
+    copies = [pltpu.make_async_copy(ocean, ocean_out, sem.at[0]), pltpu.make_async_copy(surface, surface_out, sem.at[1])]
+    for copy in copies:
+        copy.start()
+    for copy in copies:
+        copy.wait()
 
 
 def solution(mesh):
@@ -510,6 +518,16 @@
             diff_h.reshape(1, levels),
             diff_v.reshape(1, levels - 1),
         )))
+        ocean, surface = pl.pallas_call(
+            store,
+            out_shape=(
+                jax.ShapeDtypeStruct((levels, own), F32),
+                jax.ShapeDtypeStruct((tracers, atm_cells // B, B), F32),
+            ),
+            in_specs=[vm, vm],
+            out_specs=(hbm, hbm),
+            scratch_shapes=[dma((2,))],
+        )(*(pltpu.with_memory_space_constraint(x, pltpu.VMEM) for x in (ocean, surface)))
         return ocean[None], surface.reshape(tracers, 1, atm_cells)
 
     in_specs = (

time: 26.9 us -> 26.3 us (0.978)
  local copies, waits for them, and re-layouts: 1.32 us -> 0 us
  Pallas kernels: 24.7 us -> 25.5 us
    unnamed x2 -> x0, local copies, waits for them, and re-layouts: 1.32 us -> none
    pallas_call x0 -> x1, Pallas kernels: none -> 0.75 us  [local(): pl.pallas_call(store, out_shape=(jax.ShapeDtypeStruct((levels, own), F32)...]
where the time goes in v5:
time: 26.3 us; the launch traced here: 26.1 us
  Pallas kernels  25.5 us (97%)
  between operations  0.64 us (2%)
    pallas_call x1, Pallas kernels, local(): pl.pallas_call(functools.partial(kernel, nc, nt, ns, nb, levels), out_sha...  24.8 us
    pallas_call x1, Pallas kernels, local(): pl.pallas_call(store, out_shape=(jax.ShapeDtypeStruct((levels, own), F32)...  0.75 us

profile of v5, /device:TPU:8, one launch (start us, length us, event | category | flops | bytes accessed | tf_op | source)
XLA Modules:
  0.0 26.1 jit_solution(17861169807569314344)
XLA Ops:
  0.6 24.8 %shard_map.104 = (f32[80,1024]{1,0:T(8,128)S(1)}, f32[4,4,128]{2,1,0:T(4,128)S(1)}) custom-call(f32[4,4,128]{2,1,0:T(4,128)} %bitcast.10, f32[80,1024]{1,0:T(8,128)} %bitcast.9, s32[4,8]{1,0:T(4,128)} %bitcast.12, s32[1,8]{1,0:T(1,128)} %bitcast.13, f32[8,4,128,128]{3,2,1,0:T(8,128)} %weight.1, s32[6,1024]{1,0:T(8,128)} %neighbors.1, s32[8,128]{1,0:T(8,128)} %bitcast.11, ...), custom_call_target="tpu_custom_call" | custom-call | tf_op jit(solution)/shard_map/pallas_call | solution.py:457
  25.4 0.7 %shard_map.105 = (f32[80,1024]{1,0:T(8,128)}, f32[4,4,128]{2,1,0:T(4,128)}) custom-call(f32[80,1024]{1,0:T(8,128)S(1)} %get-tuple-element.6.ocean, f32[4,4,128]{2,1,0:T(4,128)S(1)} %get-tuple-element.7.surface), custom_call_target="tpu_custom_call" | custom-call | tf_op jit(solution)/shard_map/pallas_call | solution.py:521

commit v6 on v5

--- a/solution.py
+++ b/solution.py
@@ -54,15 +54,9 @@
         return pc, ps
 
     def each_peer(body):
-        for dc in sorted(range(nc), key=lambda d: -min(d, nc - d)):
-            def at(k, carry, dc=dc):
-                off = (k + 1) // 2
-                ds = lax.rem(ns // 2 + off * (1 - 2 * lax.rem(k, 2)) + ns, ns)
-                pc, ps = lax.rem(c + dc, nc), lax.rem(s + ds, ns)
-                body(pc, ps)
-                return carry
-
-            lax.fori_loop(0, ns - 1 if dc == 0 else ns, at, 0, unroll=True)
+        steps = [(dc, ds) for dc in range(nc) for ds in range(ns) if dc or ds]
+        for dc, ds in sorted(steps, key=lambda d: -min(d[0], nc - d[0]) - min(d[1], ns - d[1])):
+            body(lax.rem(c + dc, nc), lax.rem(s + ds, ns))
 
     first_slot = jnp.logical_and(slot == 0, t == 0)
     has_left, has_right = line > 0, line < nt * ns - 1

time: 26.3 us -> 26.2 us (level)
  no operation moved by 1% of the time
where the time goes in v6:
time: 26.2 us; the launch traced here: 26.1 us
  Pallas kernels  25.4 us (97%)
  between operations  0.64 us (2%)
    pallas_call x1, Pallas kernels, local(): pl.pallas_call(functools.partial(kernel, nc, nt, ns, nb, levels), out_sha...  24.7 us
    pallas_call x1, Pallas kernels, local(): pl.pallas_call(store, out_shape=(jax.ShapeDtypeStruct((levels, own), F32)...  0.75 us

profile of v6, /device:TPU:8, one launch (start us, length us, event | category | flops | bytes accessed | tf_op | source)
XLA Modules:
  0.0 26.1 jit_solution(10179649967030411992)
XLA Ops:
  0.6 24.7 %shard_map.104 = (f32[80,1024]{1,0:T(8,128)S(1)}, f32[4,4,128]{2,1,0:T(4,128)S(1)}) custom-call(f32[4,4,128]{2,1,0:T(4,128)} %bitcast.10, f32[80,1024]{1,0:T(8,128)} %bitcast.9, s32[4,8]{1,0:T(4,128)} %bitcast.12, s32[1,8]{1,0:T(1,128)} %bitcast.13, f32[8,4,128,128]{3,2,1,0:T(8,128)} %weight.1, s32[6,1024]{1,0:T(8,128)} %neighbors.1, s32[8,128]{1,0:T(8,128)} %bitcast.11, ...), custom_call_target="tpu_custom_call" | custom-call | tf_op jit(solution)/shard_map/pallas_call | solution.py:451
  25.3 0.7 %shard_map.105 = (f32[80,1024]{1,0:T(8,128)}, f32[4,4,128]{2,1,0:T(4,128)}) custom-call(f32[80,1024]{1,0:T(8,128)S(1)} %get-tuple-element.6.ocean, f32[4,4,128]{2,1,0:T(4,128)S(1)} %get-tuple-element.7.surface), custom_call_target="tpu_custom_call" | custom-call | tf_op jit(solution)/shard_map/pallas_call | solution.py:515

commit v7 on v6

--- a/solution.py
+++ b/solution.py
@@ -213,7 +213,12 @@
         d = depth[0:1, lo : lo + n]
         rows = values.shape[0]
         k = lax.broadcasted_iota(jnp.int32, (rows, n), 0)
-        hi, low = split(jnp.where(k < d, values, 0.0))
+        values = jnp.where(k < d, values, 0.0)
+        if rows == 8:
+            hi = values.astype(BF16).astype(F32)
+            store[0:16, lo : lo + n] = jnp.concatenate([hi, values - hi], 0).astype(BF16)
+            return
+        hi, low = split(values)
         store[0:rows, lo : lo + n] = hi
         store[rows : 2 * rows, lo : lo + n] = low
 
@@ -400,10 +405,6 @@
         ocean[8:levels, here] = new[8:levels]
         ocean[0:8, here] = jnp.where(k < 3, vt2[:, lo : lo + n], new[0:8])
 
-    pltpu.make_async_copy(arrived, arrived, sem_surf.at[1]).wait()
-    for i in range(nc):
-        surface[i] = jnp.sum(arrived[i * ns : (i + 1) * ns], axis=0)
-
     sent = pl.ds(0, peers - 1)
     fewer = pl.ds(0, peers - 2)
 
@@ -421,11 +422,15 @@
     def _():
         bulk.wait_send()
 
-    pltpu.make_async_copy(parts.at[sent], parts.at[sent], sem_surf.at[0]).wait()
     of_sides(
         lambda: [copy.wait_send() for copy in (halo[1], halo[3], halo[5], copies[1])] and None,
         lambda: [copy.wait_send() for copy in (halo[0], halo[2], halo[4], copies[0])] and None,
     )
+
+    pltpu.make_async_copy(arrived, arrived, sem_surf.at[1]).wait()
+    for i in range(nc):
+        surface[i] = jnp.sum(arrived[i * ns : (i + 1) * ns], axis=0)
+    pltpu.make_async_copy(parts.at[sent], parts.at[sent], sem_surf.at[0]).wait()
 
 
 def store(ocean, surface, ocean_out, surface_out, sem):

time: 26.2 us -> 26.2 us (level)
  no operation moved by 1% of the time
where the time goes in v7:
time: 26.2 us; the launch traced here: 26.1 us
  Pallas kernels  25.4 us (97%)
  between operations  0.64 us (2%)
    pallas_call x1, Pallas kernels, local(): pl.pallas_call(functools.partial(kernel, nc, nt, ns, nb, levels), out_sha...  24.7 us
    pallas_call x1, Pallas kernels, local(): pl.pallas_call(store, out_shape=(jax.ShapeDtypeStruct((levels, own), F32)...  0.75 us

profile of v7, /device:TPU:8, one launch (start us, length us, event | category | flops | bytes accessed | tf_op | source)
XLA Modules:
  0.0 26.1 jit_solution(14297547897948640054)
XLA Ops:
  0.6 24.7 %shard_map.104 = (f32[80,1024]{1,0:T(8,128)S(1)}, f32[4,4,128]{2,1,0:T(4,128)S(1)}) custom-call(f32[4,4,128]{2,1,0:T(4,128)} %bitcast.10, f32[80,1024]{1,0:T(8,128)} %bitcast.9, s32[4,8]{1,0:T(4,128)} %bitcast.12, s32[1,8]{1,0:T(1,128)} %bitcast.13, f32[8,4,128,128]{3,2,1,0:T(8,128)} %weight.1, s32[6,1024]{1,0:T(8,128)} %neighbors.1, s32[8,128]{1,0:T(8,128)} %bitcast.11, ...), custom_call_target="tpu_custom_call" | custom-call | tf_op jit(solution)/shard_map/pallas_call | solution.py:456
  25.3 0.7 %shard_map.105 = (f32[80,1024]{1,0:T(8,128)}, f32[4,4,128]{2,1,0:T(4,128)}) custom-call(f32[80,1024]{1,0:T(8,128)S(1)} %get-tuple-element.6.ocean, f32[4,4,128]{2,1,0:T(4,128)S(1)} %get-tuple-element.7.surface), custom_call_target="tpu_custom_call" | custom-call | tf_op jit(solution)/shard_map/pallas_call | solution.py:520
